TPU v7x, 256 devices: a whole 4x4x8 slice. The times are simulated.
256 devices in a mesh: ax: 4 (over z_lo), rad: 8 (over y, core), az: 8 (over x, z_hi).
Axes of the slice: x: 4, y: 4, z: 8 (z_hi: 2, z_lo: 4; z = z_hi * 4 + z_lo), core: 2. Of those that a mesh axis runs over, the one named last changes fastest.
Arguments:
- positions: float32 [3, 4, 8, 131072], P(None, 'ax', 'rad', 'az'), may hold values from 0 to 0.1
- velocity: float32 [3, 4, 8, 131072], P(None, 'ax', 'rad', 'az'), may hold values from -6 to 6
- diameter: float32 [4, 8, 131072], P('ax', 'rad', 'az'), may hold values from 0.02 to 0.1
- cell_index: int32 [4, 8, 131072], P('ax', 'rad', 'az'), may hold values from 0 to 32767
- pair_list: int32 [2, 4, 8, 262144], P(None, 'ax', 'rad', 'az'), may hold values from 0 to 34815, as said below
- live_pairs: int32 [4, 8, 8], P('ax', 'rad', 'az'), may hold values from 8192 to 32768, as said below
- gas_velocity: float32 [3, 32, 128, 2048], P(None, 'ax', 'rad', 'az'), may hold values from -6 to 6
Outputs:
- disturbance: float32 [3, 4, 8, 131072], P(None, 'ax', 'rad', 'az')
- drag_source: float32 [3, 32, 128, 2048], P(None, 'ax', 'rad', 'az')
Inputs may be any that keep to these rules, and one draw needn't show every extreme that they name: pair_list[0] is an own droplet, under 16384; a partner on a neighbouring device lies among that device's last 2048 droplets (q from 14336) or first 2048 droplets (q under 2 * 16384 + 2048); an own partner differs from the first droplet. `live_pairs`: slots at and beyond the count are padding and are ignored.
All inputs are finite; a program needn't handle non-finite values.
Results may differ from a plain program's by a relative error of at most 0.0003.
Values sent between devices are 32-bit elements; how exact they have to be, the bound alone decides.
No kernel may reach another device: no remote copies, remote signals or barrier semaphores. Data moves between devices by JAX's collectives and lax.ppermute only.
A program may use at most 128 MiB of HBM per device.

v0:
```python
import functools
import math

import jax
import jax.numpy as jnp
from jax import lax
from jax.experimental import pallas as pl
from jax.experimental.pallas import tpu as pltpu
from jax.sharding import PartitionSpec as P

piep_coef = 1.0
drag_coef = 20.0

LANES = 128
ROWS = 8
BLOCK = 2048
GAS_WINDOW = 10
HEAD_WINDOW = 10
DEAD = 1 << 29

NT = (((1,), (1,)), ((), ()))
ANY = pl.ANY
VMEM = pltpu.VMEM
SMEM = pltpu.SMEM


def params(megabytes=40):
    return pltpu.CompilerParams(vmem_limit_bytes=megabytes << 20)


def lane_gather(table, index):
    numbers = lax.GatherDimensionNumbers(
        offset_dims=(),
        collapsed_slice_dims=(1,),
        start_index_map=(1,),
        operand_batching_dims=(0,),
        start_indices_batching_dims=(0,),
    )
    return lax.gather(
        table,
        index[..., None],
        numbers,
        slice_sizes=(1, 1),
        mode=lax.GatherScatterMode.PROMISE_IN_BOUNDS,
    )


def sort_network(regs, place, levels):
    sub = lax.broadcasted_iota(jnp.int32, (ROWS, LANES), 0)
    lane = lax.broadcasted_iota(jnp.int32, (ROWS, LANES), 1)
    count = len(regs)

    def bit_fill(bit, v):
        if bit >= levels:
            return 0
        kind, k = place[bit]
        if kind == "v":
            return -((v >> k) & 1)
        return -(((sub if kind == "s" else lane) >> k) & 1)

    flip = [0] * count
    for level in range(1, levels + 1):
        fills = {}
        for v in range(count):
            kind, k = place[level] if level < levels else ("v", 99)
            key = (v >> k) & 1 if kind == "v" else 0
            if key not in fills:
                fills[key] = bit_fill(level, v)
            new = fills[key]
            if isinstance(new, int) and isinstance(flip[v], int):
                if new != flip[v]:
                    regs[v] = ~regs[v]
            else:
                regs[v] = regs[v] ^ (new ^ flip[v])
            flip[v] = new
        for bit in reversed(range(level)):
            kind, k = place[bit]
            step = 1 << k
            if kind == "v":
                for v in range(count):
                    if not v & step:
                        a, b = regs[v], regs[v | step]
                        regs[v], regs[v | step] = jnp.minimum(a, b), jnp.maximum(a, b)
            else:
                axis, size, where = (0, ROWS, sub) if kind == "s" else (1, LANES, lane)
                lower = (where & step) == 0
                for v in range(count):
                    x = regs[v]
                    ahead = pltpu.roll(x, size - step, axis)
                    behind = ahead if 2 * step == size else pltpu.roll(x, step, axis)
                    regs[v] = jnp.where(lower, jnp.minimum(x, ahead), jnp.maximum(x, behind))
    return regs


def split_two(x):
    high = x.astype(jnp.bfloat16).astype(jnp.float32)
    return high, x - high


def split_three(x):
    high, rest = split_two(x)
    mid, low = split_two(rest)
    return high, mid, low


def packed_row(ref, row):
    return jnp.broadcast_to(ref[row : row + 1, :], (16, LANES)).astype(jnp.bfloat16)


def one_hot_rows(low, count, iota16):
    one = jnp.ones((16, LANES), jnp.bfloat16)
    zero = jnp.zeros((16, LANES), jnp.bfloat16)
    return jnp.concatenate(
        [jnp.where(low - float(16 * k) == iota16, one, zero) for k in range(count // 16)], axis=0
    )


def spread_add(rel, parts, hot, iota16):
    hit = rel == iota16
    zero = jnp.zeros((16, LANES), jnp.bfloat16)
    rows = jnp.concatenate([jnp.where(hit, p, zero) for part in parts for p in part], axis=0)
    out = lax.dot_general(rows, hot, NT, preferred_element_type=jnp.float32)
    total = out[0:48]
    for s in range(1, len(parts)):
        total = total + out[48 * s : 48 * s + 48]
    return total


def row_iota():
    return lax.broadcasted_iota(jnp.int32, (16, LANES), 0).astype(jnp.float32).astype(jnp.bfloat16)


def rows_of(block):
    start = block * 16
    return pl.ds(start if isinstance(block, int) else pl.multiple_of(start, 16), 16)


def wide(ref, *at):
    return jnp.broadcast_to(ref[at[:-1] + (slice(at[-1], at[-1] + 1),)], (ROWS, LANES))


def window(table, first, count, row, low, found):
    for u in range(count):
        found = jnp.where(row == first + u, lane_gather(table[first + u], low), found)
    return found


def running_max(x, count):
    x = jnp.broadcast_to(x, (ROWS, LANES))
    step = 1
    while step < count:
        x = jnp.maximum(x, pltpu.roll(x, LANES - step, 1))
        step *= 2
    return x


def fill_gas_rows(gas_ref, gas_rows):
    for r in range(16):
        rows = slice(r * ROWS, (r + 1) * ROWS)
        for c in range(3):
            for half in range(2):
                gas_rows[rows, half * 4 + c, :] = gas_ref[c, rows, half * LANES : (half + 1) * LANES]


def gas_index(block, keys_ref, slot):
    idx = slot[0]
    keys = keys_ref[rows_of(block), :]
    idx[0] = lax.shift_right_logical(keys, 19)
    idx[1] = lax.shift_right_logical(keys, 11) & (LANES - 1)


def gas_gather(block, g, ends, gas_rows, slot):
    idx, found = slot[0], slot[1]
    zero = jnp.zeros((ROWS, LANES), jnp.float32)
    first = ends[0, block * 16 + g]
    found[g] = window(gas_rows, first, GAS_WINDOW, wide(idx, 0, g), wide(idx, 1, g), zero)


def gas_rest(block, ends, gas_rows, slot):
    idx, found = slot[0], slot[1]

    @pl.when(ends[16, block * 16] >= GAS_WINDOW)
    def _():
        def one(g, carry):
            first = ends[0, block * 16 + g]
            row = jnp.broadcast_to(idx[0, pl.ds(g, 1), :], (ROWS, LANES))
            low = jnp.broadcast_to(idx[1, pl.ds(g, 1), :], (ROWS, LANES))

            def trip(t, total):
                base = jnp.minimum(first + GAS_WINDOW * t, LANES)
                return window(gas_rows, base, GAS_WINDOW, row, low, total)

            trips = (ends[15, block * 16 + g] - first) // GAS_WINDOW + 1
            found[g] = lax.fori_loop(1, trips, trip, found[g])
            return carry

        lax.fori_loop(0, 16, one, 0)


def seen_values(block, keys_ref, slot):
    idx, found, val = slot
    keys = keys_ref[rows_of(block), :]
    upper = (keys & (1 << 18)) != 0
    place_in = keys & (BLOCK - 1)
    val[0] = lax.shift_right_logical(place_in, 7).astype(jnp.float32)
    val[1] = (place_in & (LANES - 1)).astype(jnp.float32)
    for c in range(3):
        seen = jnp.where(upper, found[:, 4 + c, :], found[:, c, :])
        for n, part in enumerate(split_three(seen)):
            val[2 + 3 * c + n] = part


def seen_in_order(g, slot, iota16):
    val = slot[2]
    rel = packed_row(val.at[0], g)
    hot = one_hot_rows(packed_row(val.at[1], g), LANES, iota16)
    parts = [[packed_row(val.at[2 + 3 * c + n], g) for c in range(3)] for n in range(3)]
    return spread_add(rel, parts, hot, iota16)


def write_states(block, total, pos_ref, vel_ref, diam_ref, out_ref, out_rows):
    rows = rows_of(block)
    for c in range(3):
        out_ref[out_rows, c, :] = pos_ref[c, rows, :]
        out_ref[out_rows, 3 + c, :] = total[16 * c : 16 * c + 16] - vel_ref[c, rows, :]
    out_ref[out_rows, 6, :] = 0.5 * diam_ref[rows, :]
    out_ref[out_rows, 7, :] = jnp.zeros((16, LANES), jnp.float32)


def states_step(gather, scatter, keys_ref, ends, gas_rows, iota16, arrays):
    total = jnp.zeros((48, LANES), jnp.float32)
    if gather:
        gas_index(gather[0], keys_ref, gather[1])
    if scatter:
        seen_values(scatter[0], keys_ref, scatter[1])
    for g in range(16):
        if gather:
            gas_gather(gather[0], g, ends, gas_rows, gather[1])
        if scatter:
            total = total + seen_in_order(g, scatter[1], iota16)
    if scatter:
        write_states(scatter[0], total, *arrays, *scatter[2:])
    if gather:
        gas_rest(gather[0], ends, gas_rows, gather[1])


def edge_states_kernel(
    cell_hbm, gas_hbm, pos_hbm, vel_hbm, diam_hbm,
    keys_ref, ends_ref, first_ref, last_ref,
    cell_ref, gas_ref, pos_ref, vel_ref, diam_ref,
    gas_rows, ends, idx_a, found_a, val_a, idx_b, found_b, val_b, sems,
):
    sources = (cell_hbm, gas_hbm, pos_hbm, vel_hbm, diam_hbm)
    places = (cell_ref, gas_ref, pos_ref, vel_ref, diam_ref)
    copies = [
        pltpu.make_async_copy(x, y, sems.at[n]) for n, (x, y) in enumerate(zip(sources, places))
    ]
    for copy in copies:
        copy.start()
    copies[0].wait()
    sub = lax.broadcasted_iota(jnp.int32, (ROWS, LANES), 0)
    lane = lax.broadcasted_iota(jnp.int32, (ROWS, LANES), 1)
    regs = []
    for v in range(16):
        own = (v % 2) * 1024 + sub * LANES + lane
        regs.append(cell_ref[v * ROWS : (v + 1) * ROWS, :] * BLOCK + own)
    place = [("l", k) for k in range(7)] + [("s", k) for k in range(3)] + [("v", 0)]
    regs = sort_network(regs, place, 11)
    keys = jnp.concatenate(regs, axis=0)
    keys_ref[...] = keys
    turned = lax.shift_right_logical(keys, 19).T
    ends_ref[0:8, :] = turned[0:8]
    ends_ref[8:16, :] = turned[120:128]
    ends_ref[16:24, :] = running_max(turned[127:128] - turned[0:1], 16)
    copy = pltpu.make_async_copy(ends_ref, ends, sems.at[5])
    copy.start()
    copies[1].wait()
    fill_gas_rows(gas_ref, gas_rows)
    for other in copies[2:]:
        other.wait()
    copy.wait()
    iota16 = row_iota()
    a, b = (idx_a, found_a, val_a), (idx_b, found_b, val_b)
    whole = slice(0, 16)
    step = functools.partial(
        states_step, keys_ref=keys_ref, ends=ends, gas_rows=gas_rows, iota16=iota16,
        arrays=(pos_ref, vel_ref, diam_ref),
    )
    step((0, a), None)
    step((7, b), (0, a, first_ref, whole))
    step(None, (7, b, last_ref, whole))


def slots(rows, parts, dtype=jnp.float32):
    one = [VMEM((2, 16, LANES), jnp.int32), VMEM((16, ROWS, LANES), dtype), VMEM((parts, rows, LANES), dtype)]
    return one + one


def edge_states(cells, gas, pos, vel, diam):
    f32, i32 = jnp.float32, jnp.int32
    arrays = (cells, gas, pos, vel, diam)
    return pl.pallas_call(
        edge_states_kernel,
        name="edge_states",
        out_shape=(
            jax.ShapeDtypeStruct((128, LANES), i32),
            jax.ShapeDtypeStruct((24, LANES), i32),
            jax.ShapeDtypeStruct((16, ROWS, LANES), f32),
            jax.ShapeDtypeStruct((16, ROWS, LANES), f32),
        ),
        in_specs=[pl.BlockSpec(memory_space=pltpu.HBM)] * 5,
        scratch_shapes=[VMEM(x.shape, x.dtype) for x in arrays]
        + [VMEM((144, ROWS, LANES), f32), SMEM((24, LANES), i32)]
        + slots(16, 11)
        + [pltpu.SemaphoreType.DMA((6,))],
        compiler_params=params(),
    )(*arrays)


def inner_states_kernel(
    ends, keys_ref, gas_ref, pos_ref, vel_ref, diam_ref, first_ref, last_ref,
    table_ref,
    gas_rows, idx_a, found_a, val_a, idx_b, found_b, val_b,
):
    fill_gas_rows(gas_ref, gas_rows)
    iota16 = row_iota()
    a, b = (idx_a, found_a, val_a), (idx_b, found_b, val_b)
    step = functools.partial(
        states_step, keys_ref=keys_ref, ends=ends, gas_rows=gas_rows, iota16=iota16,
        arrays=(pos_ref, vel_ref, diam_ref),
    )
    table_ref[0:16] = first_ref[...]
    table_ref[112:128] = last_ref[...]
    step((1, a), None)

    def two(k, carry):
        block = 2 * k + 1
        step((block + 1, b), (block, a, table_ref, rows_of(block)))
        step((jnp.minimum(block + 2, 6), a), (block + 1, b, table_ref, rows_of(block + 1)))
        return carry

    lax.fori_loop(0, 3, two, 0)


def inner_states(ends, keys, gas, pos, vel, diam, first, last):
    f32 = jnp.float32
    return pl.pallas_call(
        inner_states_kernel,
        name="inner_states",
        out_shape=jax.ShapeDtypeStruct((128, ROWS, LANES), f32),
        in_specs=[pl.BlockSpec(memory_space=SMEM)] + [pl.BlockSpec(memory_space=VMEM)] * 7,
        scratch_shapes=[VMEM((144, ROWS, LANES), f32)] + slots(16, 11),
        compiler_params=params(),
    )(ends, keys, gas, pos, vel, diam, first, last)


def pair_sort_kernel(live_ref, pairs_ref, keys_ref, ends_ref):
    live = live_ref[0, 0]
    sub = lax.broadcasted_iota(jnp.int32, (ROWS, LANES), 0)
    lane = lax.broadcasted_iota(jnp.int32, (ROWS, LANES), 1)
    regs = []
    for v in range(32):
        rows = slice(v * ROWS, (v + 1) * ROWS)
        slot = v * 1024 + sub * LANES + lane
        head = pairs_ref[0, rows, :]
        tail = pairs_ref[1, rows, :] - 7 * BLOCK
        bucket = lax.shift_right_logical(tail, 11)
        turn = -(bucket & 1) & (8 * BLOCK - 1)
        key = (bucket << 25) | ((head ^ turn) << 11) | (tail & (BLOCK - 1))
        regs.append(jnp.where(slot < live, key, DEAD))
    place = (
        [("v", k) for k in range(4)]
        + [("s", k) for k in range(3)]
        + [("v", 4)]
        + [("l", k) for k in range(7)]
    )
    regs = sort_network(regs, place, 15)
    for half in range(2):
        rows = regs[16 * half : 16 * half + 16]
        keys_ref[half] = jnp.concatenate(rows, axis=0).T
        least_head = least_tail = jnp.full((ROWS, LANES), 1 << 20, jnp.int32)
        most_head = most_tail = jnp.full((ROWS, LANES), -1, jnp.int32)
        for key in rows:
            used = key < DEAD
            bucket = lax.shift_right_logical(key, 25)
            head = lax.shift_right_logical(key, 18) & (LANES - 1)
            head = head ^ (-(bucket & 1) & (LANES - 1))
            least_head = jnp.minimum(least_head, jnp.where(used, head, 1 << 20))
            most_head = jnp.maximum(most_head, jnp.where(used, head, -1))
            least_tail = jnp.minimum(least_tail, jnp.where(used, bucket, 1 << 20))
            most_tail = jnp.maximum(most_tail, jnp.where(used, bucket, -1))
        first = 8 * half
        for n, (low, high, cap) in enumerate(
            ((least_head, most_head, LANES), (least_tail, most_tail, 10))
        ):
            low = jnp.min(low, axis=0, keepdims=True)
            high = jnp.max(high, axis=0, keepdims=True)
            ends_ref[first + 2 * n : first + 2 * n + 1, :] = jnp.minimum(low, cap)
            ends_ref[first + 2 * n + 1 : first + 2 * n + 2, :] = high
            ends_ref[first + 4 + n : first + 5 + n, :] = running_max(high - low + 1, ROWS)[0:1]
        ends_ref[first + 6 : first + 8, :] = jnp.zeros((2, LANES), jnp.int32)


def pair_sort(live, pairs):
    return pl.pallas_call(
        pair_sort_kernel,
        name="pair_sort",
        out_shape=(
            jax.ShapeDtypeStruct((2, LANES, LANES), jnp.int32),
            jax.ShapeDtypeStruct((16, LANES), jnp.int32),
        ),
        in_specs=[pl.BlockSpec(memory_space=SMEM), pl.BlockSpec(memory_space=VMEM)],
        compiler_params=params(),
    )(live, pairs)


def pair_index(number, keys_ref, slot):
    idx, val = slot[0], slot[3]
    half = number & 1
    first = pl.multiple_of((number >> 1) * ROWS, ROWS)
    keys = keys_ref[half, pl.ds(first, ROWS), :]
    used = keys < DEAD
    bucket = lax.shift_right_logical(keys, 25)
    turn = -(bucket & 1) & (8 * BLOCK - 1)
    head = (lax.shift_right_logical(keys, 11) & (8 * BLOCK - 1)) ^ turn
    head_row = jnp.where(used, lax.shift_right_logical(head, 7), -1)
    tail_row = jnp.where(used, bucket * 16 + (lax.shift_right_logical(keys, 7) & 15), -1)
    for n, x in enumerate((head_row + 16, head & (LANES - 1), tail_row, keys & (LANES - 1))):
        idx[n] = x
        val[n] = (x - 16 if n == 0 else x).astype(jnp.float32)
    val[16] = used.astype(jnp.float32)


def pair_gather(number, g, ends, table, slot):
    idx, near, far = slot[0:3]
    at = 8 * (number & 1)
    group = (number >> 1) * ROWS + g
    zero = jnp.zeros((ROWS, LANES), jnp.float32)
    first = ends[at, group] + 16
    near[g] = window(table, first, HEAD_WINDOW, wide(idx, 0, g), wide(idx, 1, g), zero)
    first = ends[at + 2, group] * 16
    far[g] = window(table, first, 16, wide(idx, 2, g), wide(idx, 3, g), zero)


def pair_gather_rest(number, ends, table, slot):
    idx, near, far = slot[0:3]
    at = 8 * (number & 1)
    start = (number >> 1) * ROWS

    @pl.when((ends[at + 4, start] > HEAD_WINDOW) | (ends[at + 5, start] > 1))
    def _():
        def one(g, carry):
            row, low, tail_row, tail_low = (
                jnp.broadcast_to(idx[n, pl.ds(g, 1), :], (ROWS, LANES)) for n in range(4)
            )
            first, most = ends[at, start + g], ends[at + 1, start + g]

            def head(t, total):
                base = jnp.minimum(first + HEAD_WINDOW * t, LANES) + 16
                return window(table, base, HEAD_WINDOW, row, low, total)

            near[g] = lax.fori_loop(1, (most - first) // HEAD_WINDOW + 1, head, near[g])

            def tail(t, total):
                return window(table, t * 16, 16, tail_row, tail_low, total)

            first, most = ends[at + 2, start + g], ends[at + 3, start + g]
            far[g] = lax.fori_loop(first + 1, most + 1, tail, far[g])
            return carry

        lax.fori_loop(0, ROWS, one, 0)


def pair_values(slot):
    near, far, val = slot[1:4]
    used = val[16]
    gap = jnp.zeros((ROWS, LANES), jnp.float32)
    for c in range(3):
        apart = far[:, c, :] - near[:, c, :]
        gap = gap + apart * apart
    far_radius, near_radius = far[:, 6, :], near[:, 6, :]
    far_ratio = far_radius * lax.rsqrt(gap + far_radius * far_radius)
    near_ratio = near_radius * lax.rsqrt(gap + near_radius * near_radius)
    weight_far = jnp.where(used > 0.0, piep_coef * far_ratio * far_ratio * far_ratio, 0.0)
    weight_near = jnp.where(used > 0.0, piep_coef * near_ratio * near_ratio * near_ratio, 0.0)
    for c in range(3):
        for n, part in enumerate(split_two(weight_far * far[:, 3 + c, :])):
            val[4 + 2 * c + n] = part
        for n, part in enumerate(split_two(weight_near * near[:, 3 + c, :])):
            val[10 + 2 * c + n] = part


def pair_add(g, base, side, slot, sums, iota16):
    val = slot[3]

    def row(n):
        if isinstance(g, int):
            return packed_row(val.at[n], g)
        return jnp.broadcast_to(val[n, pl.ds(g, 1), :], (16, LANES)).astype(jnp.bfloat16)

    rel = row(2 * side) - jnp.asarray(base, jnp.int32).astype(jnp.float32).astype(jnp.bfloat16)
    hot = one_hot_rows(row(2 * side + 1), LANES, iota16)
    parts = [[row(4 + 6 * side + 2 * c + n) for c in range(3)] for n in range(2)]
    out = spread_add(rel, parts, hot, iota16)
    for c in range(3):
        sums[c, pl.ds(base, 16), :] += out[16 * c : 16 * c + 16]


def pair_scatter(number, g, ends, slot, head_sum, tail_sum, iota16):
    at = 8 * (number & 1)
    group = (number >> 1) * ROWS + g
    pair_add(g, ends[at, group], 0, slot, head_sum, iota16)
    pair_add(g, pl.multiple_of(ends[at + 2, group] * 16, 16), 1, slot, tail_sum, iota16)


def pair_scatter_rest(number, ends, slot, head_sum, tail_sum, iota16):
    at = 8 * (number & 1)
    start = (number >> 1) * ROWS

    @pl.when((ends[at + 4, start] > 16) | (ends[at + 5, start] > 1))
    def _():
        def one(g, carry):
            first, most = ends[at, start + g], ends[at + 1, start + g]

            def head(t, carry):
                base = jnp.minimum(first + 16 * t, LANES)
                pair_add(g, base, 0, slot, head_sum, iota16)
                return carry

            lax.fori_loop(1, (most - first) // 16 + 1, head, 0)

            def tail(t, carry):
                pair_add(g, pl.multiple_of(t * 16, 16), 1, slot, tail_sum, iota16)
                return carry

            first, most = ends[at + 2, start + g], ends[at + 3, start + g]
            lax.fori_loop(first + 1, most + 1, tail, 0)
            return carry

        lax.fori_loop(0, ROWS, one, 0)


def pair_kernel(
    live_ref, ends, keys_ref, own_ref, before_ref, after_ref,
    corr_ref, lower_ref, upper_ref,
    table, head_sum, tail_sum,
    idx_a, near_a, far_a, val_a, idx_b, near_b, far_b, val_b, sems,
):
    copies = [
        pltpu.make_async_copy(before_ref, table.at[0:16], sems.at[0]),
        pltpu.make_async_copy(own_ref, table.at[16:144], sems.at[1]),
        pltpu.make_async_copy(after_ref, table.at[144:160], sems.at[2]),
    ]
    for copy in copies:
        copy.start()
    head_sum[...] = jnp.zeros_like(head_sum)
    tail_sum[...] = jnp.zeros_like(tail_sum)
    for copy in copies:
        copy.wait()
    iota16 = row_iota()
    a = (idx_a, near_a, far_a, val_a)
    b = (idx_b, near_b, far_b, val_b)
    count = 2 * ((live_ref[0, 0] + 2047) // 2048)

    def step(gather, slot, scatter, other):
        pair_index(gather, keys_ref, slot)
        if other:
            pair_values(other)
        for g in range(ROWS):
            pair_gather(gather, g, ends, table, slot)
            if other:
                pair_scatter(scatter, g, ends, other, head_sum, tail_sum, iota16)
        pair_gather_rest(gather, ends, table, slot)
        if other:
            pair_scatter_rest(scatter, ends, other, head_sum, tail_sum, iota16)

    step(jnp.int32(0), a, None, None)

    def two(k, carry):
        step(2 * k + 1, b, 2 * k, a)
        step(jnp.minimum(2 * k + 2, count - 1), a, 2 * k + 1, b)
        return carry

    lax.fori_loop(0, count // 2, two, 0)
    corr_ref[...] = head_sum[:, 0:128, :] + tail_sum[:, 16:144, :]
    lower_ref[...] = tail_sum[:, 0:16, :]
    upper_ref[...] = tail_sum[:, 144:160, :]


def pair_forces(live, ends, keys, own, before, after):
    f32, i32 = jnp.float32, jnp.int32
    smem, vmem = pl.BlockSpec(memory_space=SMEM), pl.BlockSpec(memory_space=VMEM)
    hbm = pl.BlockSpec(memory_space=ANY)
    slot = [
        VMEM((4, ROWS, LANES), i32),
        VMEM((ROWS, ROWS, LANES), f32),
        VMEM((ROWS, ROWS, LANES), f32),
        VMEM((17, ROWS, LANES), f32),
    ]
    return pl.pallas_call(
        pair_kernel,
        name="pair_forces",
        out_shape=(
            jax.ShapeDtypeStruct((3, 128, LANES), f32),
            jax.ShapeDtypeStruct((3, 16, LANES), f32),
            jax.ShapeDtypeStruct((3, 16, LANES), f32),
        ),
        in_specs=[smem, smem, vmem, hbm, hbm, hbm],
        scratch_shapes=[
            VMEM((176, ROWS, LANES), f32),
            VMEM((3, 144, LANES), f32),
            VMEM((3, 176, LANES), f32),
        ]
        + slot
        + slot
        + [pltpu.SemaphoreType.DMA((3,))],
        compiler_params=params(),
    )(live, ends, keys, own, before, after)


def force_gather(block, keys_ref, table_ref, total_ref, slot):
    force, got, val = slot
    rows = rows_of(block)
    scale = (-2.0 * drag_coef) * table_ref[rows, 6, :]
    for c in range(3):
        push = scale * (table_ref[rows, 3 + c, :] + total_ref[c, rows, :])
        force[:, c, :] = push[0:8]
        force[:, 4 + c, :] = push[8:16]
    keys = keys_ref[rows, :]
    val[0] = lax.shift_right_logical(keys, 19).astype(jnp.float32)
    val[1] = (lax.shift_right_logical(keys, 11) & (2 * LANES - 1)).astype(jnp.float32)
    inner = lax.shift_right_logical(keys, 7) & 7
    low = keys & (LANES - 1)
    tables = [force[k] for k in range(ROWS)]
    for g in range(16):
        pick = jnp.broadcast_to(inner[g : g + 1, :], (ROWS, LANES))
        at = jnp.broadcast_to(low[g : g + 1, :], (ROWS, LANES))
        found = jnp.zeros((ROWS, LANES), jnp.float32)
        for k in range(ROWS):
            found = jnp.where(pick == k, lane_gather(tables[k], at), found)
        got[g] = found
    upper = (keys & 1024) != 0
    for c in range(3):
        pushed = jnp.where(upper, got[:, 4 + c, :], got[:, c, :])
        for n, part in enumerate(split_two(pushed)):
            val[2 + 2 * c + n] = part


def force_add(g, base, slot, cells, iota16):
    val = slot[2]

    def row(n):
        if isinstance(g, int):
            return packed_row(val.at[n], g)
        return jnp.broadcast_to(val[n, pl.ds(g, 1), :], (16, LANES)).astype(jnp.bfloat16)

    rel = row(0) - base.astype(jnp.float32).astype(jnp.bfloat16)
    hot = one_hot_rows(row(1), 2 * LANES, iota16)
    parts = [[row(2 + 2 * c + n) for c in range(3)] for n in range(2)]
    out = spread_add(rel, parts, hot, iota16)
    for c in range(3):
        for half in range(2):
            part = out[16 * c : 16 * c + 16, half * LANES : (half + 1) * LANES]
            cells[2 * c + half, pl.ds(base, 16), :] += part


def force_rest(block, ends, slot, cells, iota16):
    @pl.when(ends[16, block * 16] >= 16)
    def _():
        def one(g, carry):
            first, most = ends[0, block * 16 + g], ends[15, block * 16 + g]

            def trip(t, carry):
                force_add(g, jnp.minimum(first + 16 * t, LANES), slot, cells, iota16)
                return carry

            lax.fori_loop(1, (most - first) // 16 + 1, trip, 0)
            return carry

        lax.fori_loop(0, 16, one, 0)


def deposit_step(gather, scatter, ends, keys_ref, table_ref, total_ref, cells, iota16):
    if gather:
        force_gather(gather[0], keys_ref, table_ref, total_ref, gather[1])
    if scatter:
        for g in range(16):
            force_add(g, ends[0, scatter[0] * 16 + g], scatter[1], cells, iota16)
        force_rest(scatter[0], ends, scatter[1], cells, iota16)


def inner_deposit_kernel(
    ends, keys_ref, table_ref, corr_ref,
    cells,
    force_a, got_a, val_a, force_b, got_b, val_b,
):
    cells[...] = jnp.zeros_like(cells)
    a, b = (force_a, got_a, val_a), (force_b, got_b, val_b)
    step = functools.partial(
        deposit_step, ends=ends, keys_ref=keys_ref, table_ref=table_ref, total_ref=corr_ref,
        cells=cells, iota16=row_iota(),
    )
    step((1, a), None)

    def two(k, carry):
        block = 2 * k + 1
        step((block + 1, b), (block, a))
        step((jnp.minimum(block + 2, 6), a), (block + 1, b))
        return carry

    lax.fori_loop(0, 3, two, 0)


def force_slots():
    f32 = jnp.float32
    one = [VMEM((ROWS, ROWS, LANES), f32), VMEM((16, ROWS, LANES), f32), VMEM((8, 16, LANES), f32)]
    return one + one


def inner_deposit(ends, keys, table, corr):
    smem, vmem = pl.BlockSpec(memory_space=SMEM), pl.BlockSpec(memory_space=VMEM)
    return pl.pallas_call(
        inner_deposit_kernel,
        name="inner_deposit",
        out_shape=jax.ShapeDtypeStruct((6, 144, LANES), jnp.float32),
        in_specs=[smem, vmem, vmem, vmem],
        scratch_shapes=force_slots(),
        compiler_params=params(),
    )(ends, keys, table, corr)


def edge_deposit_kernel(
    ends, keys_ref, table_ref, corr_ref, lower_ref, upper_ref, inner_ref,
    out_ref, total_ref, first_ref, last_ref,
    cells, force_a, got_a, val_a, force_b, got_b, val_b,
):
    cells[...] = inner_ref[...]
    total_ref[...] = corr_ref[...]
    total_ref[:, 0:16, :] += lower_ref[...]
    total_ref[:, 112:128, :] += upper_ref[...]
    a, b = (force_a, got_a, val_a), (force_b, got_b, val_b)
    step = functools.partial(
        deposit_step, ends=ends, keys_ref=keys_ref, table_ref=table_ref, total_ref=total_ref,
        cells=cells, iota16=row_iota(),
    )
    step((0, a), None)
    step((7, b), (0, a))
    step(None, (7, b))
    for c in range(3):
        for half in range(2):
            columns = slice(half * LANES, (half + 1) * LANES)
            out_ref[c, :, columns] = cells[2 * c + half, 0:128, :]
            first_ref[c, :, columns] = cells[2 * c + half, 0:32, :]
            last_ref[c, :, columns] = cells[2 * c + half, 96:128, :]


def edge_deposit(ends, keys, table, corr, lower, upper, inner):
    f32 = jnp.float32
    smem, vmem = pl.BlockSpec(memory_space=SMEM), pl.BlockSpec(memory_space=VMEM)
    return pl.pallas_call(
        edge_deposit_kernel,
        name="edge_deposit",
        out_shape=(
            jax.ShapeDtypeStruct((3, 128, 2 * LANES), f32),
            jax.ShapeDtypeStruct((3, 128, LANES), f32),
            jax.ShapeDtypeStruct((3, 32, 2 * LANES), f32),
            jax.ShapeDtypeStruct((3, 32, 2 * LANES), f32),
        ),
        in_specs=[smem] + [vmem] * 6,
        scratch_shapes=[VMEM((6, 144, LANES), f32)] + force_slots(),
        compiler_params=params(),
    )(ends, keys, table, corr, lower, upper, inner)


def axial_kernel(taps, cells_ref, before_ref, after_ref, out_ref, first_ref, last_ref):
    for c in range(3):
        padded = jnp.concatenate([before_ref[c], cells_ref[c], after_ref[c]], axis=0)
        total = taps[0] * padded[0:128]
        for k in range(1, 5):
            total = total + taps[k] * padded[16 * k : 16 * k + 128]
        out_ref[c] = total
        for a in range(8):
            first_ref[c, 2 * a : 2 * a + 2, :] = total[16 * a : 16 * a + 2]
            last_ref[c, 2 * a : 2 * a + 2, :] = total[16 * a + 14 : 16 * a + 16]


def radial_kernel(taps, cells_ref, before_ref, after_ref, out_ref, first_ref, last_ref, padded):
    lane = lax.broadcasted_iota(jnp.int32, (LANES, LANES), 1)
    edges = jnp.zeros((LANES, LANES), jnp.float32)
    for c in range(3):
        for a in range(8):
            padded[0:2, :] = before_ref[c, 2 * a : 2 * a + 2, :]
            padded[2:18, :] = cells_ref[c, 16 * a : 16 * a + 16, :]
            padded[18:20, :] = after_ref[c, 2 * a : 2 * a + 2, :]
            total = taps[0] * padded[0:16, :]
            for k in range(1, 5):
                total = total + taps[k] * padded[k : k + 16, :]
            out_ref[c, 16 * a : 16 * a + 16, :] = total
        left, right = out_ref[c, :, 0:LANES], out_ref[c, :, LANES:]
        if c:
            left = pltpu.roll(left, 2 * c, 1)
        right = pltpu.roll(right, 10 + 2 * c, 1)
        edges = jnp.where((lane >> 1) == c, left, edges)
        edges = jnp.where((lane >> 1) == 4 + c, right, edges)
    turned = edges.T
    first_ref[...] = turned[0:8]
    last_ref[...] = turned[8:16]


def azimuthal_kernel(taps, cells_ref, before_ref, after_ref, out_ref):
    lane = lax.broadcasted_iota(jnp.int32, (LANES, LANES), 1)
    rest = jnp.zeros((LANES - 16, LANES), jnp.float32)
    edges = jnp.concatenate([after_ref[...], before_ref[...], rest], axis=0).T
    for c in range(3):
        ahead = pltpu.roll(edges, LANES - 2 * c, 1) if c else edges
        halo = jnp.where(lane < 64, ahead, pltpu.roll(edges, 118 - 2 * c, 1))
        left, right = cells_ref[c, :, 0:LANES], cells_ref[c, :, LANES:]
        out_left, out_right = taps[2] * left, taps[2] * right
        for k in (1, 2):
            tap = taps[2 + k]
            inner = lane < LANES - k
            x, y, z = (pltpu.roll(v, LANES - k, 1) for v in (left, right, halo))
            out_left = out_left + tap * jnp.where(inner, x, y)
            out_right = out_right + tap * jnp.where(inner, y, z)
            inner = lane >= k
            x, y, z = (pltpu.roll(v, k, 1) for v in (left, right, halo))
            out_left = out_left + tap * jnp.where(inner, x, z)
            out_right = out_right + tap * jnp.where(inner, y, x)
        out_ref[c, :, 0:LANES] = out_left
        out_ref[c, :, LANES:] = out_right


def filtered(deposit, first, last):
    f32 = jnp.float32
    raw = [math.exp(-0.5 * k * k) for k in range(-2, 3)]
    taps = [x / sum(raw) for x in raw]
    whole = jax.ShapeDtypeStruct(deposit.shape, f32)
    radial_face = jax.ShapeDtypeStruct((3, 16, 2 * LANES), f32)
    edge = jax.ShapeDtypeStruct((8, LANES), f32)
    cells, first, last = pl.pallas_call(
        functools.partial(axial_kernel, taps),
        name="axial_filter",
        out_shape=(whole, radial_face, radial_face),
        compiler_params=params(),
    )(deposit, shifted(last, "ax", 1, False), shifted(first, "ax", -1, False))
    cells, first, last = pl.pallas_call(
        functools.partial(radial_kernel, taps),
        name="radial_filter",
        out_shape=(whole, edge, edge),
        scratch_shapes=[VMEM((24, 2 * LANES), f32)],
        compiler_params=params(),
    )(cells, shifted(last, "rad", 1, False), shifted(first, "rad", -1, False))
    return pl.pallas_call(
        functools.partial(azimuthal_kernel, taps),
        name="azimuthal_filter",
        out_shape=whole,
        compiler_params=params(),
    )(cells, shifted(last, "az", 1, True), shifted(first, "az", -1, True))


def shifted(x, axis, by, wrap):
    count = lax.axis_size(axis)
    pairs = [(i, (i + by) % count) for i in range(count)]
    return lax.ppermute(x, axis, [p for p in pairs if wrap or p[1] - p[0] == by])


def per_device(positions, velocity, diameter, cell_index, pair_list, live_pairs, gas_velocity):
    live = live_pairs.reshape(1, 1)
    cells = cell_index.reshape(128, LANES)
    gas = gas_velocity.reshape(3, 128, 2 * LANES)
    pos = positions.reshape(3, 128, LANES)
    vel = velocity.reshape(3, 128, LANES)
    diam = diameter.reshape(128, LANES)
    cell_keys, cell_ends, first, last = edge_states(cells, gas, pos, vel, diam)
    before = shifted(last, "az", 1, True)
    after = shifted(first, "az", -1, True)
    table = inner_states(cell_ends, cell_keys, gas, pos, vel, diam, first, last)
    pair_keys, pair_ends = pair_sort(live, pair_list.reshape(2, 256, LANES))
    corr, lower, upper = pair_forces(live, pair_ends, pair_keys, table, before, after)
    from_upper = shifted(lower, "az", -1, True)
    from_lower = shifted(upper, "az", 1, True)
    inner = inner_deposit(cell_ends, cell_keys, table, corr)
    deposit, correction, first, last = edge_deposit(
        cell_ends, cell_keys, table, corr, from_lower, from_upper, inner
    )
    smoothed = filtered(deposit, first, last)
    return (correction.reshape(positions.shape), smoothed.reshape(gas_velocity.shape))


def solution(mesh):
    return jax.shard_map(
        per_device,
        mesh=mesh,
        in_specs=(
            P(None, "ax", "rad", "az"),
            P(None, "ax", "rad", "az"),
            P("ax", "rad", "az"),
            P("ax", "rad", "az"),
            P(None, "ax", "rad", "az"),
            P("ax", "rad", "az"),
            P(None, "ax", "rad", "az"),
        ),
        out_specs=(P(None, "ax", "rad", "az"), P(None, "ax", "rad", "az")),
        check_vma=False,
    )
```

profile of v0, /device:TPU:15, one launch (start us, length us, event | category | flops | bytes accessed | tf_op | source)
XLA Modules:
  0.0 108.4 jit_solution(1730085529793608269)
XLA Ops:
  0.6 1.0 copy-done
  1.6 0.9 copy-done.2
  2.6 0.9 copy-done.4
  3.5 0.8 copy-done.6
  4.3 0.8 copy-done.8
  5.2 8.3 %edge_states.1 = (s32[128,128]{1,0:T(8,128)S(1)}, s32[24,128]{1,0:T(8,128)S(1)}, f32[16,8,128]{2,1,0:T(8,128)S(1)}, f32[16,8,128]{2,1,0:T(8,128)S(1)}) custom-call(s32[128,128]{1,0:T(8,128)S(1)} %bitcast.20, f32[3,128,256]{2,1,0:T(8,128)S(1)} %bitcast.11, f32[3,128,128]{2,1,0:T(8,128)S(1)} %bitcast.13, f32[3,128,128]{2,1,0:T(8,128)S(1)} %bitcast.15, ...), custom_call_target="tpu_custom_call" | custom-call | tf_op jit(solution)/shard_map/edge_states/pallas_call | solution.py:302
  13.5 0.0 copy-start.3
  13.5 7.2 %collective-permute-start.1 = (f32[16,8,128]{2,1,0:T(8,128)S(1)}, f32[16,8,128]{2,1,0:T(8,128)S(1)}, u32[]{:S(2)}, u32[]{:S(2)}) collective-permute-start(f32[16,8,128]{2,1,0:T(8,128)S(1)} %get-tuple-element.23.first_ref), channel_id=1, source_target_pairs={{0,7},{1,0},{2,1},{3,2},{4,3},{5,4},{6,5},{7,6},{8,15},{9,8},{10,9... | collective-permute-start | bytes 196616 | tf_op jit(solution)/shard_map/ppermute | solution.py:864
  20.7 0.0 collective-permute-start
  21.4 3.9 %pair_sort.1 = (s32[2,128,128]{2,1,0:T(8,128)S(1)}, s32[16,128]{1,0:T(8,128)S(1)}) custom-call(s32[1,1]{1,0:T(1,128)} %bitcast.9.live_ref, s32[2,256,128]{2,1,0:T(8,128)S(1)} %bitcast.19), custom_call_target="tpu_custom_call" | custom-call | tf_op jit(solution)/shard_map/pair_sort/pallas_call | solution.py:405
  25.3 7.0 %inner_states.1.own_ref.table_ref = f32[128,8,128]{2,1,0:T(8,128)S(1)} custom-call(s32[24,128]{1,0:T(8,128)S(1)} %get-tuple-element.21.ends, s32[128,128]{1,0:T(8,128)S(1)} %get-tuple-element.22.keys_ref, f32[3,128,256]{2,1,0:T(8,128)S(1)} %bitcast.12, f32[3,128,128]{2,1,0:T(8,128)S(1)} %bitcast.14, f32[3,128,128]{2,1,0:T(8,128)S(1)} %bitcast.16, ...), custom_call_target="tpu_custom_call" | custom-call | tf_op jit(solution)/shard_map/inner_states/pallas_call | solution.py:347
  32.3 0.0 collective-permute-done.1.after_ref
  32.3 25.8 %pair_forces.1 = (f32[3,128,128]{2,1,0:T(8,128)S(1)}, f32[3,16,128]{2,1,0:T(8,128)S(1)}, f32[3,16,128]{2,1,0:T(8,128)S(1)}) custom-call(s32[1,1]{1,0:T(1,128)} %bitcast.10.live_ref, s32[16,128]{1,0:T(8,128)S(1)} %get-tuple-element.25.ends, s32[2,128,128]{2,1,0:T(8,128)S(1)} %get-tuple-element.26.keys_ref, f32[128,8,128]{2,1,0:T(8,128)S(1)} %inner_states.1.own_ref.table_ref, ...), custom_call_target="tpu_custom_call" | custom-call | tf_op jit(solution)/shard_map/pair_forces/pallas_call | solution.py:600
  58.2 7.9 %collective-permute-start.2 = (f32[3,16,128]{2,1,0:T(8,128)S(1)}, f32[3,16,128]{2,1,0:T(8,128)S(1)}, u32[]{:S(2)}, u32[]{:S(2)}) collective-permute-start(f32[3,16,128]{2,1,0:T(8,128)S(1)} %get-tuple-element.28), channel_id=1, source_target_pairs={{0,1},{1,2},{2,3},{3,4},{4,5},{5,6},{6,7},{7,0},{8,9},{9,10},{10,1... | collective-permute-start | bytes 73736 | tf_op jit(solution)/shard_map/ppermute | solution.py:864
  66.0 4.2 %inner_deposit.1.inner_ref = f32[6,144,128]{2,1,0:T(8,128)S(1)} custom-call(s32[24,128]{1,0:T(8,128)S(1)} %get-tuple-element.21.ends, s32[128,128]{1,0:T(8,128)S(1)} %get-tuple-element.22.keys_ref, f32[128,8,128]{2,1,0:T(8,128)S(1)} %inner_states.1.own_ref.table_ref, f32[3,128,128]{2,1,0:T(8,128)S(1)} %get-tuple-element.27.corr_ref), custom_call_target="tpu_custom_call" | custom-call | tf_op jit(solution)/shard_map/inner_deposit/pallas_call | solution.py:722
  70.2 0.0 collective-permute-done.2.lower_ref
  70.2 2.4 %collective-permute-done.3.upper_ref = f32[3,16,128]{2,1,0:T(8,128)S(1)} collective-permute-done((f32[3,16,128]{2,1,0:T(8,128)S(1)}, f32[3,16,128]{2,1,0:T(8,128)S(1)}, u32[]{:S(2)}, u32[]{:S(2)}) %collective-permute-start.3) | collective-permute-done | bytes 24608 | tf_op jit(solution)/shard_map/ppermute | solution.py:864
  72.7 2.8 %edge_deposit.1 = (f32[3,128,256]{2,1,0:T(8,128)S(1)}, f32[3,128,128]{2,1,0:T(8,128)}, f32[3,32,256]{2,1,0:T(8,128)S(1)}, f32[3,32,256]{2,1,0:T(8,128)S(1)}) custom-call(s32[24,128]{1,0:T(8,128)S(1)} %get-tuple-element.21.ends, s32[128,128]{1,0:T(8,128)S(1)} %get-tuple-element.22.keys_ref, f32[128,8,128]{2,1,0:T(8,128)S(1)} %inner_states.1.own_ref.table_ref, ...), custom_call_target="tpu_custom_call" | custom-call | tf_op jit(solution)/shard_map/edge_deposit/pallas_call | solution.py:760
  75.4 2.4 %collective-permute-start.4 = (f32[3,32,256]{2,1,0:T(8,128)S(1)}, f32[3,32,256]{2,1,0:T(8,128)S(1)}, u32[]{:S(2)}, u32[]{:S(2)}) collective-permute-start(f32[3,32,256]{2,1,0:T(8,128)S(1)} %get-tuple-element.32), channel_id=1, source_target_pairs={{0,64},{64,128},{128,192},{1,65},{65,129},{129,193},{2,66},{66,130... | collective-permute-start | bytes 294920 | tf_op jit(solution)/shard_map/ppermute | solution.py:864
  77.9 1.3 %collective-permute-start.5 = (f32[3,32,256]{2,1,0:T(8,128)S(1)}, f32[3,32,256]{2,1,0:T(8,128)S(1)}, u32[]{:S(2)}, u32[]{:S(2)}) collective-permute-start(f32[3,32,256]{2,1,0:T(8,128)S(1)} %get-tuple-element.33), channel_id=1, source_target_pairs={{64,0},{128,64},{192,128},{65,1},{129,65},{193,129},{66,2},{130,66... | collective-permute-start | bytes 294920 | tf_op jit(solution)/shard_map/ppermute | solution.py:864
  79.2 0.3 collective-permute-done.4.before_ref
  79.5 3.7 %collective-permute-done.5.after_ref = f32[3,32,256]{2,1,0:T(8,128)S(1)} collective-permute-done((f32[3,32,256]{2,1,0:T(8,128)S(1)}, f32[3,32,256]{2,1,0:T(8,128)S(1)}, u32[]{:S(2)}, u32[]{:S(2)}) %collective-permute-start.5) | collective-permute-done | bytes 98336 | tf_op jit(solution)/shard_map/ppermute | solution.py:864
  83.2 0.1 axial_filter.1
  83.4 8.9 %collective-permute-start.6 = (f32[3,16,256]{2,1,0:T(8,128)S(1)}, f32[3,16,256]{2,1,0:T(8,128)S(1)}, u32[]{:S(2)}, u32[]{:S(2)}) collective-permute-start(f32[3,16,256]{2,1,0:T(8,128)S(1)} %get-tuple-element.35), channel_id=1, source_target_pairs={{0,8},{8,16},{16,24},{24,32},{32,40},{40,48},{48,56},{1,9},{9,17},... | collective-permute-start | bytes 147464 | tf_op jit(solution)/shard_map/ppermute | solution.py:864
  92.3 1.9 %collective-permute-start.7 = (f32[3,16,256]{2,1,0:T(8,128)S(1)}, f32[3,16,256]{2,1,0:T(8,128)S(1)}, u32[]{:S(2)}, u32[]{:S(2)}) collective-permute-start(f32[3,16,256]{2,1,0:T(8,128)S(1)} %get-tuple-element.36), channel_id=1, source_target_pairs={{8,0},{16,8},{24,16},{32,24},{40,32},{48,40},{56,48},{9,1},{17,9},... | collective-permute-start | bytes 147464 | tf_op jit(solution)/shard_map/ppermute | solution.py:864
  94.2 3.5 %collective-permute-done.7.after_ref = f32[3,16,256]{2,1,0:T(8,128)S(1)} collective-permute-done((f32[3,16,256]{2,1,0:T(8,128)S(1)}, f32[3,16,256]{2,1,0:T(8,128)S(1)}, u32[]{:S(2)}, u32[]{:S(2)}) %collective-permute-start.7) | collective-permute-done | bytes 49184 | tf_op jit(solution)/shard_map/ppermute | solution.py:864
  97.7 0.5 radial_filter.1
  98.3 2.2 %collective-permute-start.8 = (f32[8,128]{1,0:T(8,128)S(1)}, f32[8,128]{1,0:T(8,128)S(1)}, u32[]{:S(2)}, u32[]{:S(2)}) collective-permute-start(f32[8,128]{1,0:T(8,128)S(1)} %get-tuple-element.38), channel_id=1, source_target_pairs={{0,1},{1,2},{2,3},{3,4},{4,5},{5,6},{6,7},{7,0},{8,9},{9,10},{10,1... | collective-permute-start | bytes 12296 | tf_op jit(solution)/shard_map/ppermute | solution.py:864
  100.4 4.1 %collective-permute-start.9 = (f32[8,128]{1,0:T(8,128)S(1)}, f32[8,128]{1,0:T(8,128)S(1)}, u32[]{:S(2)}, u32[]{:S(2)}) collective-permute-start(f32[8,128]{1,0:T(8,128)S(1)} %get-tuple-element.39), channel_id=1, source_target_pairs={{0,7},{1,0},{2,1},{3,2},{4,3},{5,4},{6,5},{7,6},{8,15},{9,8},{10,9... | collective-permute-start | bytes 12296 | tf_op jit(solution)/shard_map/ppermute | solution.py:864
  104.6 1.0 collective-permute-done.8.before_ref
  105.6 1.2 %collective-permute-done.9.after_ref = f32[8,128]{1,0:T(8,128)S(1)} collective-permute-done((f32[8,128]{1,0:T(8,128)S(1)}, f32[8,128]{1,0:T(8,128)S(1)}, u32[]{:S(2)}, u32[]{:S(2)}) %collective-permute-start.9) | collective-permute-done | bytes 4128 | tf_op jit(solution)/shard_map/ppermute | solution.py:864
  106.8 1.6 %azimuthal_filter.1 = f32[3,128,256]{2,1,0:T(8,128)} custom-call(f32[3,128,256]{2,1,0:T(8,128)S(1)} %get-tuple-element.37.cells_ref, f32[8,128]{1,0:T(8,128)S(1)} %collective-permute-done.8.before_ref, f32[8,128]{1,0:T(8,128)S(1)} %collective-permute-done.9.after_ref), custom_call_target="tpu_custom_call" | custom-call | tf_op jit(solution)/shard_map/azimuthal_filter/pallas_call | solution.py:853
  (15 shorter events, 0.0 us)
Async XLA Ops:
  0.6 1.0 copy-start
  1.6 0.9 copy-start.2
  2.6 0.9 copy-start.4
  3.5 0.8 copy-start.6
  4.3 0.8 copy-start.8
  5.2 16.2 %copy-start.7 = (s32[2,1,1,32768]{3,2,1,0:T(1,128)S(1)}, s32[2,1,1,32768]{3,2,1,0:T(1,128)}, u32[]{:S(2)}) copy-start(s32[2,1,1,32768]{3,2,1,0:T(1,128)} %param.11) | copy-start | bytes 786436
  5.2 20.1 %copy-start.1 = (f32[3,8,16,256]{3,2,1,0:T(8,128)S(1)}, f32[3,8,16,256]{3,2,1,0:T(8,128)}, u32[]{:S(2)}) copy-start(f32[3,8,16,256]{3,2,1,0:T(8,128)} %param.13) | copy-start | bytes 1179652
  5.2 20.1 %copy-start.5 = (f32[3,1,1,16384]{3,2,1,0:T(1,128)S(1)}, f32[3,1,1,16384]{3,2,1,0:T(1,128)}, u32[]{:S(2)}) copy-start(f32[3,1,1,16384]{3,2,1,0:T(1,128)} %param.8) | copy-start | bytes 589828
  13.5 11.8 %copy-start.3 = (f32[3,1,1,16384]{3,2,1,0:T(1,128)S(1)}, f32[3,1,1,16384]{3,2,1,0:T(1,128)}, u32[]{:S(2)}) copy-start(f32[3,1,1,16384]{3,2,1,0:T(1,128)} %param.7) | copy-start | bytes 589828
  13.5 18.8 %collective-permute-start.1 = (f32[16,8,128]{2,1,0:T(8,128)S(1)}, f32[16,8,128]{2,1,0:T(8,128)S(1)}, u32[]{:S(2)}, u32[]{:S(2)}) collective-permute-start(f32[16,8,128]{2,1,0:T(8,128)S(1)} %get-tuple-element.23.first_ref), channel_id=1, source_target_pairs={{0,7},{1,0},{2,1},{3,2},{4,3},{5,4},{6,5},{7,6},{8,15},{9,8},{10,9... | collective-permute-start | bytes 196616 | tf_op jit(solution)/shard_map/ppermute | solution.py:864
  20.7 11.6 %collective-permute-start = (f32[16,8,128]{2,1,0:T(8,128)S(1)}, f32[16,8,128]{2,1,0:T(8,128)S(1)}, u32[]{:S(2)}, u32[]{:S(2)}) collective-permute-start(f32[16,8,128]{2,1,0:T(8,128)S(1)} %get-tuple-element.24.last_ref), channel_id=1, source_target_pairs={{0,1},{1,2},{2,3},{3,4},{4,5},{5,6},{6,7},{7,0},{8,9},{9,10},{10,1... | collective-permute-start | bytes 196616 | tf_op jit(solution)/shard_map/ppermute | solution.py:864
  58.2 12.1 %collective-permute-start.2 = (f32[3,16,128]{2,1,0:T(8,128)S(1)}, f32[3,16,128]{2,1,0:T(8,128)S(1)}, u32[]{:S(2)}, u32[]{:S(2)}) collective-permute-start(f32[3,16,128]{2,1,0:T(8,128)S(1)} %get-tuple-element.28), channel_id=1, source_target_pairs={{0,1},{1,2},{2,3},{3,4},{4,5},{5,6},{6,7},{7,0},{8,9},{9,10},{10,1... | collective-permute-start | bytes 73736 | tf_op jit(solution)/shard_map/ppermute | solution.py:864
  66.0 6.6 %collective-permute-start.3 = (f32[3,16,128]{2,1,0:T(8,128)S(1)}, f32[3,16,128]{2,1,0:T(8,128)S(1)}, u32[]{:S(2)}, u32[]{:S(2)}) collective-permute-start(f32[3,16,128]{2,1,0:T(8,128)S(1)} %get-tuple-element.29), channel_id=1, source_target_pairs={{0,7},{1,0},{2,1},{3,2},{4,3},{5,4},{6,5},{7,6},{8,15},{9,8},{10,9... | collective-permute-start | bytes 73736 | tf_op jit(solution)/shard_map/ppermute | solution.py:864
  75.4 4.1 %collective-permute-start.4 = (f32[3,32,256]{2,1,0:T(8,128)S(1)}, f32[3,32,256]{2,1,0:T(8,128)S(1)}, u32[]{:S(2)}, u32[]{:S(2)}) collective-permute-start(f32[3,32,256]{2,1,0:T(8,128)S(1)} %get-tuple-element.32), channel_id=1, source_target_pairs={{0,64},{64,128},{128,192},{1,65},{65,129},{129,193},{2,66},{66,130... | collective-permute-start | bytes 294920 | tf_op jit(solution)/shard_map/ppermute | solution.py:864
  77.9 5.4 %collective-permute-start.5 = (f32[3,32,256]{2,1,0:T(8,128)S(1)}, f32[3,32,256]{2,1,0:T(8,128)S(1)}, u32[]{:S(2)}, u32[]{:S(2)}) collective-permute-start(f32[3,32,256]{2,1,0:T(8,128)S(1)} %get-tuple-element.33), channel_id=1, source_target_pairs={{64,0},{128,64},{192,128},{65,1},{129,65},{193,129},{66,2},{130,66... | collective-permute-start | bytes 294920 | tf_op jit(solution)/shard_map/ppermute | solution.py:864
  83.4 10.9 %collective-permute-start.6 = (f32[3,16,256]{2,1,0:T(8,128)S(1)}, f32[3,16,256]{2,1,0:T(8,128)S(1)}, u32[]{:S(2)}, u32[]{:S(2)}) collective-permute-start(f32[3,16,256]{2,1,0:T(8,128)S(1)} %get-tuple-element.35), channel_id=1, source_target_pairs={{0,8},{8,16},{16,24},{24,32},{32,40},{40,48},{48,56},{1,9},{9,17},... | collective-permute-start | bytes 147464 | tf_op jit(solution)/shard_map/ppermute | solution.py:864
  92.3 5.4 %collective-permute-start.7 = (f32[3,16,256]{2,1,0:T(8,128)S(1)}, f32[3,16,256]{2,1,0:T(8,128)S(1)}, u32[]{:S(2)}, u32[]{:S(2)}) collective-permute-start(f32[3,16,256]{2,1,0:T(8,128)S(1)} %get-tuple-element.36), channel_id=1, source_target_pairs={{8,0},{16,8},{24,16},{32,24},{40,32},{48,40},{56,48},{9,1},{17,9},... | collective-permute-start | bytes 147464 | tf_op jit(solution)/shard_map/ppermute | solution.py:864
  98.3 7.3 %collective-permute-start.8 = (f32[8,128]{1,0:T(8,128)S(1)}, f32[8,128]{1,0:T(8,128)S(1)}, u32[]{:S(2)}, u32[]{:S(2)}) collective-permute-start(f32[8,128]{1,0:T(8,128)S(1)} %get-tuple-element.38), channel_id=1, source_target_pairs={{0,1},{1,2},{2,3},{3,4},{4,5},{5,6},{6,7},{7,0},{8,9},{9,10},{10,1... | collective-permute-start | bytes 12296 | tf_op jit(solution)/shard_map/ppermute | solution.py:864
  100.4 6.4 %collective-permute-start.9 = (f32[8,128]{1,0:T(8,128)S(1)}, f32[8,128]{1,0:T(8,128)S(1)}, u32[]{:S(2)}, u32[]{:S(2)}) collective-permute-start(f32[8,128]{1,0:T(8,128)S(1)} %get-tuple-element.39), channel_id=1, source_target_pairs={{0,7},{1,0},{2,1},{3,2},{4,3},{5,4},{6,5},{7,6},{8,15},{9,8},{10,9... | collective-permute-start | bytes 12296 | tf_op jit(solution)/shard_map/ppermute | solution.py:864
where the time goes:
time: 109 us; the launch traced here: 108 us
  Pallas kernels  54.3 us (50%)
  starting transfers between devices  36 us (33%)
  waiting for transfers between devices  12.2 us (11%)
  local copies, waits for them, and re-layouts  4.54 us (4%)
  between operations  1.44 us (1%)
    ppermute x10, starting transfers between devices, shifted(): lax.ppermute(x, axis, [p for p in pairs if wrap or p[1] - p[0] == by])  36 us
    pallas_call x1, Pallas kernels, pair_forces(): pl.pallas_call(pair_kernel, name='pair_forces', out_shape=(jax.ShapeDtype...  25.8 us
    ppermute x10, waiting for transfers between devices, shifted(): lax.ppermute(x, axis, [p for p in pairs if wrap or p[1] - p[0] == by])  12.2 us
    pallas_call x1, Pallas kernels, edge_states(): pl.pallas_call(edge_states_kernel, name='edge_states', out_shape=(jax.Sha...  8.3 us
    pallas_call x1, Pallas kernels, inner_states(): pl.pallas_call(inner_states_kernel, name='inner_states', out_shape=jax.Sh...  6.97 us
    unnamed x18, local copies, waits for them, and re-layouts  4.54 us
    pallas_call x1, Pallas kernels, inner_deposit(): pl.pallas_call(inner_deposit_kernel, name='inner_deposit', out_shape=jax....  4.18 us
    pallas_call x1, Pallas kernels, pair_sort(): pl.pallas_call(pair_sort_kernel, name='pair_sort', out_shape=(jax.ShapeDt...  3.89 us
  transfers between devices with their start and end apart: 10, of which 6 were waited for; matrix products, arithmetic and copies ran while one was open for 0% of the time, Pallas kernels for 14%

commit v1 on v0

--- a/solution.py
+++ b/solution.py
@@ -19,7 +19,6 @@
 DEAD = 1 << 29
 
 NT = (((1,), (1,)), ((), ()))
-ANY = pl.ANY
 VMEM = pltpu.VMEM
 SMEM = pltpu.SMEM
 
@@ -107,27 +106,37 @@
     return jnp.broadcast_to(ref[row : row + 1, :], (16, LANES)).astype(jnp.bfloat16)
 
 
-def one_hot_rows(low, count, iota16):
+def one_hot_rows(low, iota):
     one = jnp.ones((16, LANES), jnp.bfloat16)
     zero = jnp.zeros((16, LANES), jnp.bfloat16)
     return jnp.concatenate(
-        [jnp.where(low - float(16 * k) == iota16, one, zero) for k in range(count // 16)], axis=0
-    )
-
-
-def spread_add(rel, parts, hot, iota16):
-    hit = rel == iota16
+        [jnp.where(low == iota[k : k + 16, :], one, zero) for k in range(0, iota.shape[0], 16)],
+        axis=0,
+    )
+
+
+def spread_rows(rel, parts, iota):
+    hit = rel == iota[0:16, :]
     zero = jnp.zeros((16, LANES), jnp.bfloat16)
-    rows = jnp.concatenate([jnp.where(hit, p, zero) for part in parts for p in part], axis=0)
-    out = lax.dot_general(rows, hot, NT, preferred_element_type=jnp.float32)
+    return jnp.concatenate([jnp.where(hit, p, zero) for part in parts for p in part], axis=0)
+
+
+def spread_add(rows, hots):
+    out = lax.dot_general(
+        jnp.concatenate(rows, axis=1) if len(rows) > 1 else rows[0],
+        jnp.concatenate(hots, axis=1) if len(hots) > 1 else hots[0],
+        NT,
+        preferred_element_type=jnp.float32,
+    )
     total = out[0:48]
-    for s in range(1, len(parts)):
-        total = total + out[48 * s : 48 * s + 48]
+    for s in range(48, out.shape[0], 48):
+        total = total + out[s : s + 48]
     return total
 
 
-def row_iota():
-    return lax.broadcasted_iota(jnp.int32, (16, LANES), 0).astype(jnp.float32).astype(jnp.bfloat16)
+def fill_iota(iota):
+    rows = lax.broadcasted_iota(jnp.int32, iota.shape, 0)
+    iota[...] = rows.astype(jnp.float32).astype(jnp.bfloat16)
 
 
 def rows_of(block):
@@ -140,8 +149,9 @@
 
 
 def window(table, first, count, row, low, found):
+    rel = row - first
     for u in range(count):
-        found = jnp.where(row == first + u, lane_gather(table[first + u], low), found)
+        found = jnp.where(rel == u, lane_gather(table[first + u], low), found)
     return found
 
 
@@ -210,12 +220,14 @@
             val[2 + 3 * c + n] = part
 
 
-def seen_in_order(g, slot, iota16):
+def seen_in_order(groups, slot, iota):
     val = slot[2]
-    rel = packed_row(val.at[0], g)
-    hot = one_hot_rows(packed_row(val.at[1], g), LANES, iota16)
-    parts = [[packed_row(val.at[2 + 3 * c + n], g) for c in range(3)] for n in range(3)]
-    return spread_add(rel, parts, hot, iota16)
+    rows, hots = [], []
+    for g in groups:
+        parts = [[packed_row(val.at[2 + 3 * c + n], g) for c in range(3)] for n in range(3)]
+        rows.append(spread_rows(packed_row(val.at[0], g), parts, iota))
+        hots.append(one_hot_rows(packed_row(val.at[1], g), iota))
+    return spread_add(rows, hots)
 
 
 def write_states(block, total, pos_ref, vel_ref, diam_ref, out_ref, out_rows):
@@ -227,7 +239,7 @@
     out_ref[out_rows, 7, :] = jnp.zeros((16, LANES), jnp.float32)
 
 
-def states_step(gather, scatter, keys_ref, ends, gas_rows, iota16, arrays):
+def states_step(gather, scatter, keys_ref, ends, gas_rows, iota, arrays):
     total = jnp.zeros((48, LANES), jnp.float32)
     if gather:
         gas_index(gather[0], keys_ref, gather[1])
@@ -236,8 +248,8 @@
     for g in range(16):
         if gather:
             gas_gather(gather[0], g, ends, gas_rows, gather[1])
-        if scatter:
-            total = total + seen_in_order(g, scatter[1], iota16)
+        if scatter and g % 2:
+            total = total + seen_in_order((g - 1, g), scatter[1], iota)
     if scatter:
         write_states(scatter[0], total, *arrays, *scatter[2:])
     if gather:
@@ -248,7 +260,7 @@
     cell_hbm, gas_hbm, pos_hbm, vel_hbm, diam_hbm,
     keys_ref, ends_ref, first_ref, last_ref,
     cell_ref, gas_ref, pos_ref, vel_ref, diam_ref,
-    gas_rows, ends, idx_a, found_a, val_a, idx_b, found_b, val_b, sems,
+    gas_rows, iota, ends, idx_a, found_a, val_a, idx_b, found_b, val_b, sems,
 ):
     sources = (cell_hbm, gas_hbm, pos_hbm, vel_hbm, diam_hbm)
     places = (cell_ref, gas_ref, pos_ref, vel_ref, diam_ref)
@@ -279,11 +291,11 @@
     for other in copies[2:]:
         other.wait()
     copy.wait()
-    iota16 = row_iota()
+    fill_iota(iota)
     a, b = (idx_a, found_a, val_a), (idx_b, found_b, val_b)
     whole = slice(0, 16)
     step = functools.partial(
-        states_step, keys_ref=keys_ref, ends=ends, gas_rows=gas_rows, iota16=iota16,
+        states_step, keys_ref=keys_ref, ends=ends, gas_rows=gas_rows, iota=iota,
         arrays=(pos_ref, vel_ref, diam_ref),
     )
     step((0, a), None)
@@ -310,23 +322,23 @@
         ),
         in_specs=[pl.BlockSpec(memory_space=pltpu.HBM)] * 5,
         scratch_shapes=[VMEM(x.shape, x.dtype) for x in arrays]
-        + [VMEM((144, ROWS, LANES), f32), SMEM((24, LANES), i32)]
+        + [VMEM((144, ROWS, LANES), f32), VMEM((LANES, LANES), jnp.bfloat16), SMEM((24, LANES), i32)]
         + slots(16, 11)
         + [pltpu.SemaphoreType.DMA((6,))],
-        compiler_params=params(),
+        compiler_params=params(60),
     )(*arrays)
 
 
 def inner_states_kernel(
     ends, keys_ref, gas_ref, pos_ref, vel_ref, diam_ref, first_ref, last_ref,
     table_ref,
-    gas_rows, idx_a, found_a, val_a, idx_b, found_b, val_b,
+    gas_rows, iota, idx_a, found_a, val_a, idx_b, found_b, val_b,
 ):
     fill_gas_rows(gas_ref, gas_rows)
-    iota16 = row_iota()
+    fill_iota(iota)
     a, b = (idx_a, found_a, val_a), (idx_b, found_b, val_b)
     step = functools.partial(
-        states_step, keys_ref=keys_ref, ends=ends, gas_rows=gas_rows, iota16=iota16,
+        states_step, keys_ref=keys_ref, ends=ends, gas_rows=gas_rows, iota=iota,
         arrays=(pos_ref, vel_ref, diam_ref),
     )
     table_ref[0:16] = first_ref[...]
@@ -349,7 +361,8 @@
         name="inner_states",
         out_shape=jax.ShapeDtypeStruct((128, ROWS, LANES), f32),
         in_specs=[pl.BlockSpec(memory_space=SMEM)] + [pl.BlockSpec(memory_space=VMEM)] * 7,
-        scratch_shapes=[VMEM((144, ROWS, LANES), f32)] + slots(16, 11),
+        scratch_shapes=[VMEM((144, ROWS, LANES), f32), VMEM((LANES, LANES), jnp.bfloat16)]
+        + slots(16, 11),
         compiler_params=params(),
     )(ends, keys, gas, pos, vel, diam, first, last)
 
@@ -398,7 +411,7 @@
             ends_ref[first + 2 * n : first + 2 * n + 1, :] = jnp.minimum(low, cap)
             ends_ref[first + 2 * n + 1 : first + 2 * n + 2, :] = high
             ends_ref[first + 4 + n : first + 5 + n, :] = running_max(high - low + 1, ROWS)[0:1]
-        ends_ref[first + 6 : first + 8, :] = jnp.zeros((2, LANES), jnp.int32)
+        ends_ref[first + 6 : first + 8, :] = running_max(high, ROWS)[0:2]
 
 
 def pair_sort(live, pairs):
@@ -490,7 +503,7 @@
             val[10 + 2 * c + n] = part
 
 
-def pair_add(g, base, side, slot, sums, iota16):
+def pair_rows(g, base, side, slot, iota):
     val = slot[3]
 
     def row(n):
@@ -499,65 +512,72 @@
         return jnp.broadcast_to(val[n, pl.ds(g, 1), :], (16, LANES)).astype(jnp.bfloat16)
 
     rel = row(2 * side) - jnp.asarray(base, jnp.int32).astype(jnp.float32).astype(jnp.bfloat16)
-    hot = one_hot_rows(row(2 * side + 1), LANES, iota16)
     parts = [[row(4 + 6 * side + 2 * c + n) for c in range(3)] for n in range(2)]
-    out = spread_add(rel, parts, hot, iota16)
+    return spread_rows(rel, parts, iota), one_hot_rows(row(2 * side + 1), iota)
+
+
+def add_rows(sums, base, out):
     for c in range(3):
         sums[c, pl.ds(base, 16), :] += out[16 * c : 16 * c + 16]
 
 
-def pair_scatter(number, g, ends, slot, head_sum, tail_sum, iota16):
-    at = 8 * (number & 1)
-    group = (number >> 1) * ROWS + g
-    pair_add(g, ends[at, group], 0, slot, head_sum, iota16)
-    pair_add(g, pl.multiple_of(ends[at + 2, group] * 16, 16), 1, slot, tail_sum, iota16)
-
-
-def pair_scatter_rest(number, ends, slot, head_sum, tail_sum, iota16):
+def pair_add_heads(g, base, slot, head_sum, iota):
+    rows, hot = pair_rows(g, base, 0, slot, iota)
+    add_rows(head_sum, base, spread_add([rows], [hot]))
+
+
+def pair_add_tails(groups, bucket, slot, tail_sum, iota):
+    base = pl.multiple_of(bucket * 16, 16)
+    pieces = [pair_rows(g, base, 1, slot, iota) for g in groups]
+    add_rows(tail_sum, base, spread_add([p[0] for p in pieces], [p[1] for p in pieces]))
+
+
+def pair_scatter(number, g, ends, slot, head_sum, tail_sum, iota):
     at = 8 * (number & 1)
     start = (number >> 1) * ROWS
-
-    @pl.when((ends[at + 4, start] > 16) | (ends[at + 5, start] > 1))
+    pair_add_heads(g, ends[at, start + g], slot, head_sum, iota)
+    if g % 4 == 3:
+        pair_add_tails(range(g - 3, g + 1), ends[at + 2, start], slot, tail_sum, iota)
+
+
+def pair_scatter_rest(number, ends, slot, head_sum, tail_sum, iota):
+    at = 8 * (number & 1)
+    start = (number >> 1) * ROWS
+
+    @pl.when(ends[at + 4, start] > 16)
     def _():
         def one(g, carry):
             first, most = ends[at, start + g], ends[at + 1, start + g]
 
             def head(t, carry):
-                base = jnp.minimum(first + 16 * t, LANES)
-                pair_add(g, base, 0, slot, head_sum, iota16)
+                pair_add_heads(g, jnp.minimum(first + 16 * t, LANES), slot, head_sum, iota)
                 return carry
 
             lax.fori_loop(1, (most - first) // 16 + 1, head, 0)
-
-            def tail(t, carry):
-                pair_add(g, pl.multiple_of(t * 16, 16), 1, slot, tail_sum, iota16)
-                return carry
-
-            first, most = ends[at + 2, start + g], ends[at + 3, start + g]
-            lax.fori_loop(first + 1, most + 1, tail, 0)
             return carry
 
         lax.fori_loop(0, ROWS, one, 0)
+
+    def tail(bucket, carry):
+        pair_add_tails(range(0, 4), bucket, slot, tail_sum, iota)
+        pair_add_tails(range(4, 8), bucket, slot, tail_sum, iota)
+        return carry
+
+    lax.fori_loop(ends[at + 2, start] + 1, ends[at + 6, start] + 1, tail, 0)
 
 
 def pair_kernel(
     live_ref, ends, keys_ref, own_ref, before_ref, after_ref,
     corr_ref, lower_ref, upper_ref,
-    table, head_sum, tail_sum,
-    idx_a, near_a, far_a, val_a, idx_b, near_b, far_b, val_b, sems,
+    table, head_sum, tail_sum, iota,
+    idx_a, near_a, far_a, val_a, idx_b, near_b, far_b, val_b,
 ):
-    copies = [
-        pltpu.make_async_copy(before_ref, table.at[0:16], sems.at[0]),
-        pltpu.make_async_copy(own_ref, table.at[16:144], sems.at[1]),
-        pltpu.make_async_copy(after_ref, table.at[144:160], sems.at[2]),
-    ]
-    for copy in copies:
-        copy.start()
+    table[0:16] = before_ref[...]
+    table[16:144] = own_ref[...]
+    table[144:160] = after_ref[...]
     head_sum[...] = jnp.zeros_like(head_sum)
     tail_sum[...] = jnp.zeros_like(tail_sum)
-    for copy in copies:
-        copy.wait()
-    iota16 = row_iota()
+    fill_iota(iota)
     a = (idx_a, near_a, far_a, val_a)
     b = (idx_b, near_b, far_b, val_b)
     count = 2 * ((live_ref[0, 0] + 2047) // 2048)
@@ -569,10 +589,10 @@
         for g in range(ROWS):
             pair_gather(gather, g, ends, table, slot)
             if other:
-                pair_scatter(scatter, g, ends, other, head_sum, tail_sum, iota16)
+                pair_scatter(scatter, g, ends, other, head_sum, tail_sum, iota)
         pair_gather_rest(gather, ends, table, slot)
         if other:
-            pair_scatter_rest(scatter, ends, other, head_sum, tail_sum, iota16)
+            pair_scatter_rest(scatter, ends, other, head_sum, tail_sum, iota)
 
     step(jnp.int32(0), a, None, None)
 
@@ -590,7 +610,6 @@
 def pair_forces(live, ends, keys, own, before, after):
     f32, i32 = jnp.float32, jnp.int32
     smem, vmem = pl.BlockSpec(memory_space=SMEM), pl.BlockSpec(memory_space=VMEM)
-    hbm = pl.BlockSpec(memory_space=ANY)
     slot = [
         VMEM((4, ROWS, LANES), i32),
         VMEM((ROWS, ROWS, LANES), f32),
@@ -605,15 +624,15 @@
             jax.ShapeDtypeStruct((3, 16, LANES), f32),
             jax.ShapeDtypeStruct((3, 16, LANES), f32),
         ),
-        in_specs=[smem, smem, vmem, hbm, hbm, hbm],
+        in_specs=[smem, smem, vmem, vmem, vmem, vmem],
         scratch_shapes=[
             VMEM((176, ROWS, LANES), f32),
             VMEM((3, 144, LANES), f32),
             VMEM((3, 176, LANES), f32),
+            VMEM((LANES, LANES), jnp.bfloat16),
         ]
         + slot
-        + slot
-        + [pltpu.SemaphoreType.DMA((3,))],
+        + slot,
         compiler_params=params(),
     )(live, ends, keys, own, before, after)
 
@@ -646,7 +665,7 @@
             val[2 + 2 * c + n] = part
 
 
-def force_add(g, base, slot, cells, iota16):
+def force_add(g, base, slot, cells, iota):
     val = slot[2]
 
     def row(n):
@@ -655,23 +674,22 @@
         return jnp.broadcast_to(val[n, pl.ds(g, 1), :], (16, LANES)).astype(jnp.bfloat16)
 
     rel = row(0) - base.astype(jnp.float32).astype(jnp.bfloat16)
-    hot = one_hot_rows(row(1), 2 * LANES, iota16)
     parts = [[row(2 + 2 * c + n) for c in range(3)] for n in range(2)]
-    out = spread_add(rel, parts, hot, iota16)
+    out = spread_add([spread_rows(rel, parts, iota)], [one_hot_rows(row(1), iota)])
     for c in range(3):
         for half in range(2):
             part = out[16 * c : 16 * c + 16, half * LANES : (half + 1) * LANES]
             cells[2 * c + half, pl.ds(base, 16), :] += part
 
 
-def force_rest(block, ends, slot, cells, iota16):
+def force_rest(block, ends, slot, cells, iota):
     @pl.when(ends[16, block * 16] >= 16)
     def _():
         def one(g, carry):
             first, most = ends[0, block * 16 + g], ends[15, block * 16 + g]
 
             def trip(t, carry):
-                force_add(g, jnp.minimum(first + 16 * t, LANES), slot, cells, iota16)
+                force_add(g, jnp.minimum(first + 16 * t, LANES), slot, cells, iota)
                 return carry
 
             lax.fori_loop(1, (most - first) // 16 + 1, trip, 0)
@@ -680,25 +698,26 @@
         lax.fori_loop(0, 16, one, 0)
 
 
-def deposit_step(gather, scatter, ends, keys_ref, table_ref, total_ref, cells, iota16):
+def deposit_step(gather, scatter, ends, keys_ref, table_ref, total_ref, cells, iota):
     if gather:
         force_gather(gather[0], keys_ref, table_ref, total_ref, gather[1])
     if scatter:
         for g in range(16):
-            force_add(g, ends[0, scatter[0] * 16 + g], scatter[1], cells, iota16)
-        force_rest(scatter[0], ends, scatter[1], cells, iota16)
+            force_add(g, ends[0, scatter[0] * 16 + g], scatter[1], cells, iota)
+        force_rest(scatter[0], ends, scatter[1], cells, iota)
 
 
 def inner_deposit_kernel(
     ends, keys_ref, table_ref, corr_ref,
     cells,
-    force_a, got_a, val_a, force_b, got_b, val_b,
+    iota, force_a, got_a, val_a, force_b, got_b, val_b,
 ):
+    fill_iota(iota)
     cells[...] = jnp.zeros_like(cells)
     a, b = (force_a, got_a, val_a), (force_b, got_b, val_b)
     step = functools.partial(
         deposit_step, ends=ends, keys_ref=keys_ref, table_ref=table_ref, total_ref=corr_ref,
-        cells=cells, iota16=row_iota(),
+        cells=cells, iota=iota,
     )
     step((1, a), None)
 
@@ -714,7 +733,7 @@
 def force_slots():
     f32 = jnp.float32
     one = [VMEM((ROWS, ROWS, LANES), f32), VMEM((16, ROWS, LANES), f32), VMEM((8, 16, LANES), f32)]
-    return one + one
+    return [VMEM((2 * LANES, LANES), jnp.bfloat16)] + one + one
 
 
 def inner_deposit(ends, keys, table, corr):
@@ -732,8 +751,9 @@
 def edge_deposit_kernel(
     ends, keys_ref, table_ref, corr_ref, lower_ref, upper_ref, inner_ref,
     out_ref, total_ref, first_ref, last_ref,
-    cells, force_a, got_a, val_a, force_b, got_b, val_b,
+    cells, iota, force_a, got_a, val_a, force_b, got_b, val_b,
 ):
+    fill_iota(iota)
     cells[...] = inner_ref[...]
     total_ref[...] = corr_ref[...]
     total_ref[:, 0:16, :] += lower_ref[...]
@@ -741,7 +761,7 @@
     a, b = (force_a, got_a, val_a), (force_b, got_b, val_b)
     step = functools.partial(
         deposit_step, ends=ends, keys_ref=keys_ref, table_ref=table_ref, total_ref=total_ref,
-        cells=cells, iota16=row_iota(),
+        cells=cells, iota=iota,
     )
     step((0, a), None)
     step((7, b), (0, a))

time: 109 us -> 104 us (0.954)
  the two profiles are of different devices: /device:TPU:15 before, /device:TPU:40 now
where the time goes in v1:
time: 104 us; the launch traced here: 103 us
  Pallas kernels  52.6 us (51%)
  starting transfers between devices  36.4 us (35%)
  waiting for transfers between devices  10.4 us (10%)
  local copies, waits for them, and re-layouts  1.71 us (2%)
  between operations  1.52 us (1%)
    ppermute x10, starting transfers between devices, shifted(): lax.ppermute(x, axis, [p for p in pairs if wrap or p[1] - p[0] == by])  36.4 us
    pallas_call x1, Pallas kernels, pair_forces(): pl.pallas_call(pair_kernel, name='pair_forces', out_shape=(jax.ShapeDtype...  26.4 us
    ppermute x10, waiting for transfers between devices, shifted(): lax.ppermute(x, axis, [p for p in pairs if wrap or p[1] - p[0] == by])  10.4 us
    pallas_call x1, Pallas kernels, edge_states(): pl.pallas_call(edge_states_kernel, name='edge_states', out_shape=(jax.Sha...  7.89 us
    pallas_call x1, Pallas kernels, inner_states(): pl.pallas_call(inner_states_kernel, name='inner_states', out_shape=jax.Sh...  5.16 us
    pallas_call x1, Pallas kernels, inner_deposit(): pl.pallas_call(inner_deposit_kernel, name='inner_deposit', out_shape=jax....  4.11 us
    pallas_call x1, Pallas kernels, pair_sort(): pl.pallas_call(pair_sort_kernel, name='pair_sort', out_shape=(jax.ShapeDt...  3.94 us
    pallas_call x1, Pallas kernels, edge_deposit(): pl.pallas_call(edge_deposit_kernel, name='edge_deposit', out_shape=(jax.S...  2.82 us
  transfers between devices with their start and end apart: 10, of which 6 were waited for; matrix products, arithmetic and copies ran while one was open for 0% of the time, Pallas kernels for 13%

profile of v1, /device:TPU:40, one launch (start us, length us, event | category | flops | bytes accessed | tf_op | source)
XLA Modules:
  0.0 102.7 jit_solution(11105251038024163776)
XLA Ops:
  0.7 7.9 %edge_states.1 = (s32[128,128]{1,0:T(8,128)}, s32[24,128]{1,0:T(8,128)}, f32[16,8,128]{2,1,0:T(8,128)}, f32[16,8,128]{2,1,0:T(8,128)}) custom-call(s32[128,128]{1,0:T(8,128)} %bitcast.21, f32[3,128,256]{2,1,0:T(8,128)} %bitcast.11, f32[3,128,128]{2,1,0:T(8,128)} %bitcast.13, f32[3,128,128]{2,1,0:T(8,128)} %bitcast.15, f32[128,128]{1,0:T(8,128)} %bitcast.17), custom_call_target="tpu_custom_call" | custom-call | tf_op jit(solution)/shard_map/edge_states/pallas_call | solution.py:314
  8.6 0.0 copy-start.1
  8.6 8.6 %collective-permute-start.1 = (f32[16,8,128]{2,1,0:T(8,128)}, f32[16,8,128]{2,1,0:T(8,128)S(1)}, u32[]{:S(2)}, u32[]{:S(2)}) collective-permute-start(f32[16,8,128]{2,1,0:T(8,128)} %get-tuple-element.23.first_ref), channel_id=1, source_target_pairs={{0,7},{1,0},{2,1},{3,2},{4,3},{5,4},{6,5},{7,6},{8,15},{9,8},{10,9... | collective-permute-start | bytes 196616 | tf_op jit(solution)/shard_map/ppermute | solution.py:884
  17.1 0.0 collective-permute-start
  17.8 0.0 copy-start.3
  17.8 3.9 %pair_sort.1 = (s32[2,128,128]{2,1,0:T(8,128)S(1)}, s32[16,128]{1,0:T(8,128)S(1)}) custom-call(s32[1,1]{1,0:T(1,128)} %bitcast.9.live_ref, s32[2,256,128]{2,1,0:T(8,128)S(1)} %bitcast.19), custom_call_target="tpu_custom_call" | custom-call | tf_op jit(solution)/shard_map/pair_sort/pallas_call | solution.py:418
  21.8 0.8 copy-done.7
  22.7 0.8 copy-done.8
  23.5 5.2 %inner_states.1.own_ref.table_ref = f32[128,8,128]{2,1,0:T(8,128)S(1)} custom-call(s32[24,128]{1,0:T(8,128)S(1)} %copy-done.6, s32[128,128]{1,0:T(8,128)S(1)} %copy-done.3, f32[3,128,256]{2,1,0:T(8,128)S(1)} %bitcast.12, f32[3,128,128]{2,1,0:T(8,128)S(1)} %bitcast.14, f32[3,128,128]{2,1,0:T(8,128)S(1)} %bitcast.16, f32[128,128]{1,0:T(8,128)S(1)} %bitcast.18, ...), custom_call_target="tpu_custom_call" | custom-call | tf_op jit(solution)/shard_map/inner_states/pallas_call | solution.py:359
  28.7 0.0 collective-permute-done.before_ref
  28.7 26.4 %pair_forces.1 = (f32[3,128,128]{2,1,0:T(8,128)S(1)}, f32[3,16,128]{2,1,0:T(8,128)S(1)}, f32[3,16,128]{2,1,0:T(8,128)S(1)}) custom-call(s32[1,1]{1,0:T(1,128)} %bitcast.10.live_ref, s32[16,128]{1,0:T(8,128)S(1)} %get-tuple-element.25.ends, s32[2,128,128]{2,1,0:T(8,128)S(1)} %get-tuple-element.26.keys_ref, f32[128,8,128]{2,1,0:T(8,128)S(1)} %inner_states.1.own_ref.table_ref, ...), custom_call_target="tpu_custom_call" | custom-call | tf_op jit(solution)/shard_map/pair_forces/pallas_call | solution.py:619
  55.1 5.5 %collective-permute-start.2 = (f32[3,16,128]{2,1,0:T(8,128)S(1)}, f32[3,16,128]{2,1,0:T(8,128)S(1)}, u32[]{:S(2)}, u32[]{:S(2)}) collective-permute-start(f32[3,16,128]{2,1,0:T(8,128)S(1)} %get-tuple-element.28), channel_id=1, source_target_pairs={{0,1},{1,2},{2,3},{3,4},{4,5},{5,6},{6,7},{7,0},{8,9},{9,10},{10,1... | collective-permute-start | bytes 73736 | tf_op jit(solution)/shard_map/ppermute | solution.py:884
  60.5 2.9 %collective-permute-start.3 = (f32[3,16,128]{2,1,0:T(8,128)S(1)}, f32[3,16,128]{2,1,0:T(8,128)S(1)}, u32[]{:S(2)}, u32[]{:S(2)}) collective-permute-start(f32[3,16,128]{2,1,0:T(8,128)S(1)} %get-tuple-element.29), channel_id=1, source_target_pairs={{0,7},{1,0},{2,1},{3,2},{4,3},{5,4},{6,5},{7,6},{8,15},{9,8},{10,9... | collective-permute-start | bytes 73736 | tf_op jit(solution)/shard_map/ppermute | solution.py:884
  63.5 4.1 %inner_deposit.1.inner_ref = f32[6,144,128]{2,1,0:T(8,128)S(1)} custom-call(s32[24,128]{1,0:T(8,128)S(1)} %copy-done.6, s32[128,128]{1,0:T(8,128)S(1)} %copy-done.3, f32[128,8,128]{2,1,0:T(8,128)S(1)} %inner_states.1.own_ref.table_ref, f32[3,128,128]{2,1,0:T(8,128)S(1)} %get-tuple-element.27.corr_ref), custom_call_target="tpu_custom_call" | custom-call | tf_op jit(solution)/shard_map/inner_deposit/pallas_call | solution.py:741
  67.6 0.0 collective-permute-done.2.lower_ref
  67.6 0.7 collective-permute-done.3.upper_ref
  68.3 2.8 %edge_deposit.1 = (f32[3,128,256]{2,1,0:T(8,128)S(1)}, f32[3,128,128]{2,1,0:T(8,128)}, f32[3,32,256]{2,1,0:T(8,128)S(1)}, f32[3,32,256]{2,1,0:T(8,128)S(1)}) custom-call(s32[24,128]{1,0:T(8,128)S(1)} %copy-done.6, s32[128,128]{1,0:T(8,128)S(1)} %copy-done.3, f32[128,8,128]{2,1,0:T(8,128)S(1)} %inner_states.1.own_ref.table_ref, ...), custom_call_target="tpu_custom_call" | custom-call | tf_op jit(solution)/shard_map/edge_deposit/pallas_call | solution.py:780
  71.1 3.1 %collective-permute-start.4 = (f32[3,32,256]{2,1,0:T(8,128)S(1)}, f32[3,32,256]{2,1,0:T(8,128)S(1)}, u32[]{:S(2)}, u32[]{:S(2)}) collective-permute-start(f32[3,32,256]{2,1,0:T(8,128)S(1)} %get-tuple-element.32), channel_id=1, source_target_pairs={{0,64},{64,128},{128,192},{1,65},{65,129},{129,193},{2,66},{66,130... | collective-permute-start | bytes 294920 | tf_op jit(solution)/shard_map/ppermute | solution.py:884
  74.2 2.8 %collective-permute-start.5 = (f32[3,32,256]{2,1,0:T(8,128)S(1)}, f32[3,32,256]{2,1,0:T(8,128)S(1)}, u32[]{:S(2)}, u32[]{:S(2)}) collective-permute-start(f32[3,32,256]{2,1,0:T(8,128)S(1)} %get-tuple-element.33), channel_id=1, source_target_pairs={{64,0},{128,64},{192,128},{65,1},{129,65},{193,129},{66,2},{130,66... | collective-permute-start | bytes 294920 | tf_op jit(solution)/shard_map/ppermute | solution.py:884
  76.9 0.7 collective-permute-done.4.before_ref
  77.6 3.1 %collective-permute-done.5.after_ref = f32[3,32,256]{2,1,0:T(8,128)S(1)} collective-permute-done((f32[3,32,256]{2,1,0:T(8,128)S(1)}, f32[3,32,256]{2,1,0:T(8,128)S(1)}, u32[]{:S(2)}, u32[]{:S(2)}) %collective-permute-start.5) | collective-permute-done | bytes 98336 | tf_op jit(solution)/shard_map/ppermute | solution.py:884
  80.7 0.1 axial_filter.1
  80.8 1.9 %collective-permute-start.6 = (f32[3,16,256]{2,1,0:T(8,128)S(1)}, f32[3,16,256]{2,1,0:T(8,128)S(1)}, u32[]{:S(2)}, u32[]{:S(2)}) collective-permute-start(f32[3,16,256]{2,1,0:T(8,128)S(1)} %get-tuple-element.35), channel_id=1, source_target_pairs={{0,8},{8,16},{16,24},{24,32},{32,40},{40,48},{48,56},{1,9},{9,17},... | collective-permute-start | bytes 147464 | tf_op jit(solution)/shard_map/ppermute | solution.py:884
  82.7 3.6 %collective-permute-start.7 = (f32[3,16,256]{2,1,0:T(8,128)S(1)}, f32[3,16,256]{2,1,0:T(8,128)S(1)}, u32[]{:S(2)}, u32[]{:S(2)}) collective-permute-start(f32[3,16,256]{2,1,0:T(8,128)S(1)} %get-tuple-element.36), channel_id=1, source_target_pairs={{8,0},{16,8},{24,16},{32,24},{40,32},{48,40},{56,48},{9,1},{17,9},... | collective-permute-start | bytes 147464 | tf_op jit(solution)/shard_map/ppermute | solution.py:884
  86.4 0.0 collective-permute-done.6.before_ref
  86.4 2.0 %collective-permute-done.7.after_ref = f32[3,16,256]{2,1,0:T(8,128)S(1)} collective-permute-done((f32[3,16,256]{2,1,0:T(8,128)S(1)}, f32[3,16,256]{2,1,0:T(8,128)S(1)}, u32[]{:S(2)}, u32[]{:S(2)}) %collective-permute-start.7) | collective-permute-done | bytes 49184 | tf_op jit(solution)/shard_map/ppermute | solution.py:884
  88.4 0.5 radial_filter.1
  88.9 4.6 %collective-permute-start.8 = (f32[8,128]{1,0:T(8,128)S(1)}, f32[8,128]{1,0:T(8,128)S(1)}, u32[]{:S(2)}, u32[]{:S(2)}) collective-permute-start(f32[8,128]{1,0:T(8,128)S(1)} %get-tuple-element.38), channel_id=1, source_target_pairs={{0,1},{1,2},{2,3},{3,4},{4,5},{5,6},{6,7},{7,0},{8,9},{9,10},{10,1... | collective-permute-start | bytes 12296 | tf_op jit(solution)/shard_map/ppermute | solution.py:884
  93.5 3.5 %collective-permute-start.9 = (f32[8,128]{1,0:T(8,128)S(1)}, f32[8,128]{1,0:T(8,128)S(1)}, u32[]{:S(2)}, u32[]{:S(2)}) collective-permute-start(f32[8,128]{1,0:T(8,128)S(1)} %get-tuple-element.39), channel_id=1, source_target_pairs={{0,7},{1,0},{2,1},{3,2},{4,3},{5,4},{6,5},{7,6},{8,15},{9,8},{10,9... | collective-permute-start | bytes 12296 | tf_op jit(solution)/shard_map/ppermute | solution.py:884
  97.0 1.6 %collective-permute-done.8.before_ref = f32[8,128]{1,0:T(8,128)S(1)} collective-permute-done((f32[8,128]{1,0:T(8,128)S(1)}, f32[8,128]{1,0:T(8,128)S(1)}, u32[]{:S(2)}, u32[]{:S(2)}) %collective-permute-start.8) | collective-permute-done | bytes 4128 | tf_op jit(solution)/shard_map/ppermute | solution.py:884
  98.6 2.4 %collective-permute-done.9.after_ref = f32[8,128]{1,0:T(8,128)S(1)} collective-permute-done((f32[8,128]{1,0:T(8,128)S(1)}, f32[8,128]{1,0:T(8,128)S(1)}, u32[]{:S(2)}, u32[]{:S(2)}) %collective-permute-start.9) | collective-permute-done | bytes 4128 | tf_op jit(solution)/shard_map/ppermute | solution.py:884
  101.0 1.6 %azimuthal_filter.1 = f32[3,128,256]{2,1,0:T(8,128)} custom-call(f32[3,128,256]{2,1,0:T(8,128)S(1)} %get-tuple-element.37.cells_ref, f32[8,128]{1,0:T(8,128)S(1)} %collective-permute-done.8.before_ref, f32[8,128]{1,0:T(8,128)S(1)} %collective-permute-done.9.after_ref), custom_call_target="tpu_custom_call" | custom-call | tf_op jit(solution)/shard_map/azimuthal_filter/pallas_call | solution.py:873
  (15 shorter events, 0.0 us)
Async XLA Ops:
  0.6 17.2 %copy-start.5 = (s32[2,1,1,32768]{3,2,1,0:T(1,128)S(1)}, s32[2,1,1,32768]{3,2,1,0:T(1,128)}, u32[]{:S(2)}) copy-start(s32[2,1,1,32768]{3,2,1,0:T(1,128)} %param.11) | copy-start | bytes 786436
  0.6 21.1 %copy-start = (f32[3,8,16,256]{3,2,1,0:T(8,128)S(1)}, f32[3,8,16,256]{3,2,1,0:T(8,128)}, u32[]{:S(2)}) copy-start(f32[3,8,16,256]{3,2,1,0:T(8,128)} %param.13) | copy-start | bytes 1179652
  0.7 21.1 %copy-start.2 = (f32[3,1,1,16384]{3,2,1,0:T(1,128)S(1)}, f32[3,1,1,16384]{3,2,1,0:T(1,128)}, u32[]{:S(2)}) copy-start(f32[3,1,1,16384]{3,2,1,0:T(1,128)} %param.8) | copy-start | bytes 589828
  0.7 21.1 %copy-start.4 = (f32[1,1,16384]{2,1,0:T(1,128)S(1)}, f32[1,1,16384]{2,1,0:T(1,128)}, u32[]{:S(2)}) copy-start(f32[1,1,16384]{2,1,0:T(1,128)} %param.9) | copy-start | bytes 196612
  8.6 13.2 %copy-start.1 = (f32[3,1,1,16384]{3,2,1,0:T(1,128)S(1)}, f32[3,1,1,16384]{3,2,1,0:T(1,128)}, u32[]{:S(2)}) copy-start(f32[3,1,1,16384]{3,2,1,0:T(1,128)} %param.7) | copy-start | bytes 589828
  8.6 20.1 %collective-permute-start.1 = (f32[16,8,128]{2,1,0:T(8,128)}, f32[16,8,128]{2,1,0:T(8,128)S(1)}, u32[]{:S(2)}, u32[]{:S(2)}) collective-permute-start(f32[16,8,128]{2,1,0:T(8,128)} %get-tuple-element.23.first_ref), channel_id=1, source_target_pairs={{0,7},{1,0},{2,1},{3,2},{4,3},{5,4},{6,5},{7,6},{8,15},{9,8},{10,9... | collective-permute-start | bytes 196616 | tf_op jit(solution)/shard_map/ppermute | solution.py:884
  17.1 11.6 %collective-permute-start = (f32[16,8,128]{2,1,0:T(8,128)}, f32[16,8,128]{2,1,0:T(8,128)S(1)}, u32[]{:S(2)}, u32[]{:S(2)}) collective-permute-start(f32[16,8,128]{2,1,0:T(8,128)} %get-tuple-element.24.last_ref), channel_id=1, source_target_pairs={{0,1},{1,2},{2,3},{3,4},{4,5},{5,6},{6,7},{7,0},{8,9},{9,10},{10,1... | collective-permute-start | bytes 196616 | tf_op jit(solution)/shard_map/ppermute | solution.py:884
  17.8 4.0 %copy-start.3 = (s32[128,128]{1,0:T(8,128)S(1)}, s32[128,128]{1,0:T(8,128)}, u32[]{:S(2)}) copy-start(s32[128,128]{1,0:T(8,128)} %get-tuple-element.22.keys_ref) | copy-start | bytes 196612
  17.8 4.0 %copy-start.6 = (s32[24,128]{1,0:T(8,128)S(1)}, s32[24,128]{1,0:T(8,128)}, u32[]{:S(2)}) copy-start(s32[24,128]{1,0:T(8,128)} %get-tuple-element.21.ends) | copy-start | bytes 36868
  21.8 0.8 copy-start.7
  22.7 0.8 copy-start.8
  55.1 12.5 %collective-permute-start.2 = (f32[3,16,128]{2,1,0:T(8,128)S(1)}, f32[3,16,128]{2,1,0:T(8,128)S(1)}, u32[]{:S(2)}, u32[]{:S(2)}) collective-permute-start(f32[3,16,128]{2,1,0:T(8,128)S(1)} %get-tuple-element.28), channel_id=1, source_target_pairs={{0,1},{1,2},{2,3},{3,4},{4,5},{5,6},{6,7},{7,0},{8,9},{9,10},{10,1... | collective-permute-start | bytes 73736 | tf_op jit(solution)/shard_map/ppermute | solution.py:884
  60.5 7.7 %collective-permute-start.3 = (f32[3,16,128]{2,1,0:T(8,128)S(1)}, f32[3,16,128]{2,1,0:T(8,128)S(1)}, u32[]{:S(2)}, u32[]{:S(2)}) collective-permute-start(f32[3,16,128]{2,1,0:T(8,128)S(1)} %get-tuple-element.29), channel_id=1, source_target_pairs={{0,7},{1,0},{2,1},{3,2},{4,3},{5,4},{6,5},{7,6},{8,15},{9,8},{10,9... | collective-permute-start | bytes 73736 | tf_op jit(solution)/shard_map/ppermute | solution.py:884
  71.1 6.5 %collective-permute-start.4 = (f32[3,32,256]{2,1,0:T(8,128)S(1)}, f32[3,32,256]{2,1,0:T(8,128)S(1)}, u32[]{:S(2)}, u32[]{:S(2)}) collective-permute-start(f32[3,32,256]{2,1,0:T(8,128)S(1)} %get-tuple-element.32), channel_id=1, source_target_pairs={{0,64},{64,128},{128,192},{1,65},{65,129},{129,193},{2,66},{66,130... | collective-permute-start | bytes 294920 | tf_op jit(solution)/shard_map/ppermute | solution.py:884
  74.2 6.5 %collective-permute-start.5 = (f32[3,32,256]{2,1,0:T(8,128)S(1)}, f32[3,32,256]{2,1,0:T(8,128)S(1)}, u32[]{:S(2)}, u32[]{:S(2)}) collective-permute-start(f32[3,32,256]{2,1,0:T(8,128)S(1)} %get-tuple-element.33), channel_id=1, source_target_pairs={{64,0},{128,64},{192,128},{65,1},{129,65},{193,129},{66,2},{130,66... | collective-permute-start | bytes 294920 | tf_op jit(solution)/shard_map/ppermute | solution.py:884
  80.8 5.6 %collective-permute-start.6 = (f32[3,16,256]{2,1,0:T(8,128)S(1)}, f32[3,16,256]{2,1,0:T(8,128)S(1)}, u32[]{:S(2)}, u32[]{:S(2)}) collective-permute-start(f32[3,16,256]{2,1,0:T(8,128)S(1)} %get-tuple-element.35), channel_id=1, source_target_pairs={{0,8},{8,16},{16,24},{24,32},{32,40},{40,48},{48,56},{1,9},{9,17},... | collective-permute-start | bytes 147464 | tf_op jit(solution)/shard_map/ppermute | solution.py:884
  82.7 5.6 %collective-permute-start.7 = (f32[3,16,256]{2,1,0:T(8,128)S(1)}, f32[3,16,256]{2,1,0:T(8,128)S(1)}, u32[]{:S(2)}, u32[]{:S(2)}) collective-permute-start(f32[3,16,256]{2,1,0:T(8,128)S(1)} %get-tuple-element.36), channel_id=1, source_target_pairs={{8,0},{16,8},{24,16},{32,24},{40,32},{48,40},{56,48},{9,1},{17,9},... | collective-permute-start | bytes 147464 | tf_op jit(solution)/shard_map/ppermute | solution.py:884
  88.9 9.7 %collective-permute-start.8 = (f32[8,128]{1,0:T(8,128)S(1)}, f32[8,128]{1,0:T(8,128)S(1)}, u32[]{:S(2)}, u32[]{:S(2)}) collective-permute-start(f32[8,128]{1,0:T(8,128)S(1)} %get-tuple-element.38), channel_id=1, source_target_pairs={{0,1},{1,2},{2,3},{3,4},{4,5},{5,6},{6,7},{7,0},{8,9},{9,10},{10,1... | collective-permute-start | bytes 12296 | tf_op jit(solution)/shard_map/ppermute | solution.py:884
  93.5 7.5 %collective-permute-start.9 = (f32[8,128]{1,0:T(8,128)S(1)}, f32[8,128]{1,0:T(8,128)S(1)}, u32[]{:S(2)}, u32[]{:S(2)}) collective-permute-start(f32[8,128]{1,0:T(8,128)S(1)} %get-tuple-element.39), channel_id=1, source_target_pairs={{0,7},{1,0},{2,1},{3,2},{4,3},{5,4},{6,5},{7,6},{8,15},{9,8},{10,9... | collective-permute-start | bytes 12296 | tf_op jit(solution)/shard_map/ppermute | solution.py:884

commit v2 on v1

--- a/solution.py
+++ b/solution.py
@@ -15,6 +15,8 @@
 ROWS = 8
 BLOCK = 2048
 GAS_WINDOW = 10
+BUCKET = 1024
+BUCKETS = 20
 HEAD_WINDOW = 10
 DEAD = 1 << 29
 
@@ -377,9 +379,13 @@
         slot = v * 1024 + sub * LANES + lane
         head = pairs_ref[0, rows, :]
         tail = pairs_ref[1, rows, :] - 7 * BLOCK
-        bucket = lax.shift_right_logical(tail, 11)
+        own = tail - BLOCK
+        inside = (own >= 0) & (own < 8 * BLOCK)
+        tail = jnp.where(inside, jnp.maximum(own, head) + BLOCK, tail)
+        head = jnp.where(inside, jnp.minimum(own, head), head)
+        bucket = lax.shift_right_logical(tail, 10)
         turn = -(bucket & 1) & (8 * BLOCK - 1)
-        key = (bucket << 25) | ((head ^ turn) << 11) | (tail & (BLOCK - 1))
+        key = (bucket << 24) | ((head ^ turn) << 10) | (tail & (BUCKET - 1))
         regs.append(jnp.where(slot < live, key, DEAD))
     place = (
         [("v", k) for k in range(4)]
@@ -395,23 +401,18 @@
         most_head = most_tail = jnp.full((ROWS, LANES), -1, jnp.int32)
         for key in rows:
             used = key < DEAD
-            bucket = lax.shift_right_logical(key, 25)
-            head = lax.shift_right_logical(key, 18) & (LANES - 1)
+            bucket = lax.shift_right_logical(key, 24)
+            head = lax.shift_right_logical(key, 17) & (LANES - 1)
             head = head ^ (-(bucket & 1) & (LANES - 1))
             least_head = jnp.minimum(least_head, jnp.where(used, head, 1 << 20))
             most_head = jnp.maximum(most_head, jnp.where(used, head, -1))
             least_tail = jnp.minimum(least_tail, jnp.where(used, bucket, 1 << 20))
             most_tail = jnp.maximum(most_tail, jnp.where(used, bucket, -1))
-        first = 8 * half
-        for n, (low, high, cap) in enumerate(
-            ((least_head, most_head, LANES), (least_tail, most_tail, 10))
-        ):
-            low = jnp.min(low, axis=0, keepdims=True)
-            high = jnp.max(high, axis=0, keepdims=True)
-            ends_ref[first + 2 * n : first + 2 * n + 1, :] = jnp.minimum(low, cap)
-            ends_ref[first + 2 * n + 1 : first + 2 * n + 2, :] = high
-            ends_ref[first + 4 + n : first + 5 + n, :] = running_max(high - low + 1, ROWS)[0:1]
-        ends_ref[first + 6 : first + 8, :] = running_max(high, ROWS)[0:2]
+        for n, x in enumerate((least_head, most_head, least_tail, most_tail)):
+            reduce = jnp.max if n % 2 else jnp.min
+            row = 4 * half + n
+            bound = (LANES, LANES, BUCKETS, BUCKETS)[n]
+            ends_ref[row : row + 1, :] = jnp.minimum(reduce(x, axis=0, keepdims=True), bound)
 
 
 def pair_sort(live, pairs):
@@ -420,73 +421,68 @@
         name="pair_sort",
         out_shape=(
             jax.ShapeDtypeStruct((2, LANES, LANES), jnp.int32),
-            jax.ShapeDtypeStruct((16, LANES), jnp.int32),
+            jax.ShapeDtypeStruct((ROWS, LANES), jnp.int32),
         ),
         in_specs=[pl.BlockSpec(memory_space=SMEM), pl.BlockSpec(memory_space=VMEM)],
         compiler_params=params(),
     )(live, pairs)
 
 
-def pair_index(number, keys_ref, slot):
-    idx, val = slot[0], slot[3]
-    half = number & 1
-    first = pl.multiple_of((number >> 1) * ROWS, ROWS)
-    keys = keys_ref[half, pl.ds(first, ROWS), :]
+def take_items(state, groups, ends):
+    items = []
+    for _ in range(ROWS):
+        g, bucket, head = state
+        valid = g < groups
+        seen = jnp.minimum(g, 2 * LANES - 1)
+        at, lane = 4 * (seen & 1), seen >> 1
+        items.append((seen, jnp.where(valid, bucket, -1), head, bucket * 8))
+        more_heads = head + HEAD_WINDOW <= ends[at + 1, lane]
+        more_tails = bucket < ends[at + 3, lane]
+        step = jnp.where(more_heads | more_tails, 0, 1)
+        g = jnp.minimum(g + step, 2 * LANES)
+        seen = jnp.minimum(g, 2 * LANES - 1)
+        at, lane = 4 * (seen & 1), seen >> 1
+        head = jnp.where(more_heads, head + HEAD_WINDOW, ends[at, lane])
+        same = jnp.where(more_heads, bucket, bucket + 1)
+        bucket = jnp.where(step == 1, ends[at + 2, lane], same)
+        state = (g, bucket, head)
+    return items, state
+
+
+def pair_gather(k, item, keys_ref, table, slot):
+    key_rows, rel_rows, near, far = slot[0:4]
+    g, bucket, first, tail_first = item
+    keys = jnp.broadcast_to(keys_ref[g & 1, pl.ds(g >> 1, 1), :], (ROWS, LANES))
+    of_bucket = lax.shift_right_logical(keys, 24)
+    turn = -(of_bucket & 1) & (8 * BLOCK - 1)
+    head = (lax.shift_right_logical(keys, 10) & (8 * BLOCK - 1)) ^ turn
+    rel = lax.shift_right_logical(head, 7) - first
+    tail_row = lax.shift_right_logical(keys, 7) & 7
+    used = (of_bucket == bucket) & (rel >= 0) & (rel < HEAD_WINDOW)
+    key_rows[k : k + 1, :] = jnp.where(used, keys, DEAD)[0:1]
+    rel_rows[k : k + 1, :] = rel[0:1]
+    zero = jnp.zeros((ROWS, LANES), jnp.float32)
+    low = head & (LANES - 1)
+    found = zero
+    for u in range(HEAD_WINDOW):
+        found = jnp.where(rel == u, lane_gather(table[16 + first + u], low), found)
+    near[k] = found
+    low = keys & (LANES - 1)
+    found = zero
+    for u in range(8):
+        found = jnp.where(tail_row == u, lane_gather(table[tail_first + u], low), found)
+    far[k] = found
+
+
+def pair_values(slot):
+    key_rows, rel_rows, near, far, val = slot
+    keys = key_rows[...]
     used = keys < DEAD
-    bucket = lax.shift_right_logical(keys, 25)
-    turn = -(bucket & 1) & (8 * BLOCK - 1)
-    head = (lax.shift_right_logical(keys, 11) & (8 * BLOCK - 1)) ^ turn
-    head_row = jnp.where(used, lax.shift_right_logical(head, 7), -1)
-    tail_row = jnp.where(used, bucket * 16 + (lax.shift_right_logical(keys, 7) & 15), -1)
-    for n, x in enumerate((head_row + 16, head & (LANES - 1), tail_row, keys & (LANES - 1))):
-        idx[n] = x
-        val[n] = (x - 16 if n == 0 else x).astype(jnp.float32)
-    val[16] = used.astype(jnp.float32)
-
-
-def pair_gather(number, g, ends, table, slot):
-    idx, near, far = slot[0:3]
-    at = 8 * (number & 1)
-    group = (number >> 1) * ROWS + g
-    zero = jnp.zeros((ROWS, LANES), jnp.float32)
-    first = ends[at, group] + 16
-    near[g] = window(table, first, HEAD_WINDOW, wide(idx, 0, g), wide(idx, 1, g), zero)
-    first = ends[at + 2, group] * 16
-    far[g] = window(table, first, 16, wide(idx, 2, g), wide(idx, 3, g), zero)
-
-
-def pair_gather_rest(number, ends, table, slot):
-    idx, near, far = slot[0:3]
-    at = 8 * (number & 1)
-    start = (number >> 1) * ROWS
-
-    @pl.when((ends[at + 4, start] > HEAD_WINDOW) | (ends[at + 5, start] > 1))
-    def _():
-        def one(g, carry):
-            row, low, tail_row, tail_low = (
-                jnp.broadcast_to(idx[n, pl.ds(g, 1), :], (ROWS, LANES)) for n in range(4)
-            )
-            first, most = ends[at, start + g], ends[at + 1, start + g]
-
-            def head(t, total):
-                base = jnp.minimum(first + HEAD_WINDOW * t, LANES) + 16
-                return window(table, base, HEAD_WINDOW, row, low, total)
-
-            near[g] = lax.fori_loop(1, (most - first) // HEAD_WINDOW + 1, head, near[g])
-
-            def tail(t, total):
-                return window(table, t * 16, 16, tail_row, tail_low, total)
-
-            first, most = ends[at + 2, start + g], ends[at + 3, start + g]
-            far[g] = lax.fori_loop(first + 1, most + 1, tail, far[g])
-            return carry
-
-        lax.fori_loop(0, ROWS, one, 0)
-
-
-def pair_values(slot):
-    near, far, val = slot[1:4]
-    used = val[16]
+    turn = -(lax.shift_right_logical(keys, 24) & 1) & (LANES - 1)
+    val[0] = rel_rows[...].astype(jnp.float32)
+    val[1] = ((lax.shift_right_logical(keys, 10) & (LANES - 1)) ^ turn).astype(jnp.float32)
+    val[2] = (lax.shift_right_logical(keys, 7) & 7).astype(jnp.float32)
+    val[3] = (keys & (LANES - 1)).astype(jnp.float32)
     gap = jnp.zeros((ROWS, LANES), jnp.float32)
     for c in range(3):
         apart = far[:, c, :] - near[:, c, :]
@@ -494,114 +490,79 @@
     far_radius, near_radius = far[:, 6, :], near[:, 6, :]
     far_ratio = far_radius * lax.rsqrt(gap + far_radius * far_radius)
     near_ratio = near_radius * lax.rsqrt(gap + near_radius * near_radius)
-    weight_far = jnp.where(used > 0.0, piep_coef * far_ratio * far_ratio * far_ratio, 0.0)
-    weight_near = jnp.where(used > 0.0, piep_coef * near_ratio * near_ratio * near_ratio, 0.0)
+    weight_far = jnp.where(used, piep_coef * far_ratio * far_ratio * far_ratio, 0.0)
+    weight_near = jnp.where(used, piep_coef * near_ratio * near_ratio * near_ratio, 0.0)
     for c in range(3):
         for n, part in enumerate(split_two(weight_far * far[:, 3 + c, :])):
-            val[4 + 2 * c + n] = part
+            val[4 + 3 * n + c] = part
         for n, part in enumerate(split_two(weight_near * near[:, 3 + c, :])):
-            val[10 + 2 * c + n] = part
-
-
-def pair_rows(g, base, side, slot, iota):
-    val = slot[3]
-
-    def row(n):
-        if isinstance(g, int):
-            return packed_row(val.at[n], g)
-        return jnp.broadcast_to(val[n, pl.ds(g, 1), :], (16, LANES)).astype(jnp.bfloat16)
-
-    rel = row(2 * side) - jnp.asarray(base, jnp.int32).astype(jnp.float32).astype(jnp.bfloat16)
-    parts = [[row(4 + 6 * side + 2 * c + n) for c in range(3)] for n in range(2)]
-    return spread_rows(rel, parts, iota), one_hot_rows(row(2 * side + 1), iota)
-
-
-def add_rows(sums, base, out):
-    for c in range(3):
-        sums[c, pl.ds(base, 16), :] += out[16 * c : 16 * c + 16]
-
-
-def pair_add_heads(g, base, slot, head_sum, iota):
-    rows, hot = pair_rows(g, base, 0, slot, iota)
-    add_rows(head_sum, base, spread_add([rows], [hot]))
-
-
-def pair_add_tails(groups, bucket, slot, tail_sum, iota):
-    base = pl.multiple_of(bucket * 16, 16)
-    pieces = [pair_rows(g, base, 1, slot, iota) for g in groups]
-    add_rows(tail_sum, base, spread_add([p[0] for p in pieces], [p[1] for p in pieces]))
-
-
-def pair_scatter(number, g, ends, slot, head_sum, tail_sum, iota):
-    at = 8 * (number & 1)
-    start = (number >> 1) * ROWS
-    pair_add_heads(g, ends[at, start + g], slot, head_sum, iota)
-    if g % 4 == 3:
-        pair_add_tails(range(g - 3, g + 1), ends[at + 2, start], slot, tail_sum, iota)
-
-
-def pair_scatter_rest(number, ends, slot, head_sum, tail_sum, iota):
-    at = 8 * (number & 1)
-    start = (number >> 1) * ROWS
-
-    @pl.when(ends[at + 4, start] > 16)
-    def _():
-        def one(g, carry):
-            first, most = ends[at, start + g], ends[at + 1, start + g]
-
-            def head(t, carry):
-                pair_add_heads(g, jnp.minimum(first + 16 * t, LANES), slot, head_sum, iota)
-                return carry
-
-            lax.fori_loop(1, (most - first) // 16 + 1, head, 0)
-            return carry
-
-        lax.fori_loop(0, ROWS, one, 0)
-
-    def tail(bucket, carry):
-        pair_add_tails(range(0, 4), bucket, slot, tail_sum, iota)
-        pair_add_tails(range(4, 8), bucket, slot, tail_sum, iota)
-        return carry
-
-    lax.fori_loop(ends[at + 2, start] + 1, ends[at + 6, start] + 1, tail, 0)
+            val[10 + 3 * n + c] = part
+
+
+def pair_scatter(k, item, slot, head_sum, tail_sum, iota, iota8):
+    val = slot[4]
+    first, tail_first = item
+    parts = [[packed_row(val.at[4 + 3 * n + c], k) for c in range(3)] for n in range(2)]
+    rows = spread_rows(packed_row(val.at[0], k), parts, iota)
+    out = spread_add([rows], [one_hot_rows(packed_row(val.at[1], k), iota)])
+    for c in range(3):
+        head_sum[c, pl.ds(first, 16), :] += out[16 * c : 16 * c + 16]
+
+    hit = packed_row(val.at[2], k) == iota8[...]
+    zero = jnp.zeros((16, LANES), jnp.bfloat16)
+    tiles = []
+    for n in range(10, 16, 2):
+        both = jnp.concatenate([wide(val, n, k), wide(val, n + 1, k)], axis=0)
+        tiles.append(jnp.where(hit, both.astype(jnp.bfloat16), zero))
+    out = lax.dot_general(
+        jnp.concatenate(tiles, axis=0),
+        one_hot_rows(packed_row(val.at[3], k), iota),
+        NT,
+        preferred_element_type=jnp.float32,
+    )
+    at = pl.ds(pl.multiple_of(tail_first, 8), 8)
+    for c in range(3):
+        tail_sum[c, at, :] += out[8 * c : 8 * c + 8] + out[24 + 8 * c : 32 + 8 * c]
 
 
 def pair_kernel(
     live_ref, ends, keys_ref, own_ref, before_ref, after_ref,
     corr_ref, lower_ref, upper_ref,
-    table, head_sum, tail_sum, iota,
-    idx_a, near_a, far_a, val_a, idx_b, near_b, far_b, val_b,
+    table, head_sum, tail_sum, iota, iota8,
+    key_a, rel_a, near_a, far_a, val_a, key_b, rel_b, near_b, far_b, val_b,
 ):
     table[0:16] = before_ref[...]
     table[16:144] = own_ref[...]
     table[144:160] = after_ref[...]
+    table[160:168] = jnp.zeros((8, ROWS, LANES), jnp.float32)
     head_sum[...] = jnp.zeros_like(head_sum)
     tail_sum[...] = jnp.zeros_like(tail_sum)
     fill_iota(iota)
-    a = (idx_a, near_a, far_a, val_a)
-    b = (idx_b, near_b, far_b, val_b)
-    count = 2 * ((live_ref[0, 0] + 2047) // 2048)
-
-    def step(gather, slot, scatter, other):
-        pair_index(gather, keys_ref, slot)
+    rows = lax.broadcasted_iota(jnp.int32, iota8.shape, 0) & 7
+    iota8[...] = rows.astype(jnp.float32).astype(jnp.bfloat16)
+    a = (key_a, rel_a, near_a, far_a, val_a)
+    b = (key_b, rel_b, near_b, far_b, val_b)
+    groups = (live_ref[0, 0] + LANES - 1) // LANES
+
+    def step(state, slot, pending, other):
+        items, state = take_items(state, groups, ends)
         if other:
             pair_values(other)
-        for g in range(ROWS):
-            pair_gather(gather, g, ends, table, slot)
+        for k in range(ROWS):
+            pair_gather(k, items[k], keys_ref, table, slot)
             if other:
-                pair_scatter(scatter, g, ends, other, head_sum, tail_sum, iota)
-        pair_gather_rest(gather, ends, table, slot)
-        if other:
-            pair_scatter_rest(scatter, ends, other, head_sum, tail_sum, iota)
-
-    step(jnp.int32(0), a, None, None)
-
-    def two(k, carry):
-        step(2 * k + 1, b, 2 * k, a)
-        step(jnp.minimum(2 * k + 2, count - 1), a, 2 * k + 1, b)
-        return carry
-
-    lax.fori_loop(0, count // 2, two, 0)
+                pair_scatter(k, pending[k], other, head_sum, tail_sum, iota, iota8)
+        return tuple(item[2:4] for item in items), state, items[0][1] >= 0
+
+    start = (jnp.int32(0), ends[2, 0], ends[0, 0])
+    carry = step(start, a, None, None)
+
+    def two(carry):
+        pending, state, _ = carry
+        pending, state, _ = step(state, b, pending, a)
+        return step(state, a, pending, b)
+
+    lax.while_loop(lambda carry: carry[2], two, carry)
     corr_ref[...] = head_sum[:, 0:128, :] + tail_sum[:, 16:144, :]
     lower_ref[...] = tail_sum[:, 0:16, :]
     upper_ref[...] = tail_sum[:, 144:160, :]
@@ -611,10 +572,11 @@
     f32, i32 = jnp.float32, jnp.int32
     smem, vmem = pl.BlockSpec(memory_space=SMEM), pl.BlockSpec(memory_space=VMEM)
     slot = [
-        VMEM((4, ROWS, LANES), i32),
+        VMEM((ROWS, LANES), i32),
+        VMEM((ROWS, LANES), i32),
         VMEM((ROWS, ROWS, LANES), f32),
         VMEM((ROWS, ROWS, LANES), f32),
-        VMEM((17, ROWS, LANES), f32),
+        VMEM((16, ROWS, LANES), f32),
     ]
     return pl.pallas_call(
         pair_kernel,
@@ -626,10 +588,11 @@
         ),
         in_specs=[smem, smem, vmem, vmem, vmem, vmem],
         scratch_shapes=[
-            VMEM((176, ROWS, LANES), f32),
+            VMEM((168, ROWS, LANES), f32),
             VMEM((3, 144, LANES), f32),
-            VMEM((3, 176, LANES), f32),
+            VMEM((3, 168, LANES), f32),
             VMEM((LANES, LANES), jnp.bfloat16),
+            VMEM((16, LANES), jnp.bfloat16),
         ]
         + slot
         + slot,

time: 104 us -> 93.9 us (0.903)
  the two profiles are of different devices: /device:TPU:40 before, /device:TPU:7 now
where the time goes in v2:
time: 93.9 us; the launch traced here: 93 us
  Pallas kernels  44.6 us (47%)
  starting transfers between devices  33.2 us (35%)
  waiting for transfers between devices  12 us (13%)
  local copies, waits for them, and re-layouts  1.71 us (2%)
  between operations  1.51 us (2%)
    ppermute x10, starting transfers between devices, shifted(): lax.ppermute(x, axis, [p for p in pairs if wrap or p[1] - p[0] == by])  33.2 us
    pallas_call x1, Pallas kernels, pair_forces(): pl.pallas_call(pair_kernel, name='pair_forces', out_shape=(jax.ShapeDtype...  18.1 us
    ppermute x10, waiting for transfers between devices, shifted(): lax.ppermute(x, axis, [p for p in pairs if wrap or p[1] - p[0] == by])  12 us
    pallas_call x1, Pallas kernels, edge_states(): pl.pallas_call(edge_states_kernel, name='edge_states', out_shape=(jax.Sha...  7.89 us
    pallas_call x1, Pallas kernels, inner_states(): pl.pallas_call(inner_states_kernel, name='inner_states', out_shape=jax.Sh...  5.67 us
    pallas_call x1, Pallas kernels, inner_deposit(): pl.pallas_call(inner_deposit_kernel, name='inner_deposit', out_shape=jax....  4.1 us
    pallas_call x1, Pallas kernels, pair_sort(): pl.pallas_call(pair_sort_kernel, name='pair_sort', out_shape=(jax.ShapeDt...  3.78 us
    pallas_call x1, Pallas kernels, edge_deposit(): pl.pallas_call(edge_deposit_kernel, name='edge_deposit', out_shape=(jax.S...  2.82 us
  transfers between devices with their start and end apart: 10, of which 6 were waited for; matrix products, arithmetic and copies ran while one was open for 0% of the time, Pallas kernels for 15%

profile of v2, /device:TPU:7, one launch (start us, length us, event | category | flops | bytes accessed | tf_op | source)
XLA Modules:
  0.0 93.0 jit_solution(7404259681760929390)
XLA Ops:
  0.7 7.9 %edge_states.1 = (s32[128,128]{1,0:T(8,128)}, s32[24,128]{1,0:T(8,128)}, f32[16,8,128]{2,1,0:T(8,128)}, f32[16,8,128]{2,1,0:T(8,128)}) custom-call(s32[128,128]{1,0:T(8,128)} %bitcast.21, f32[3,128,256]{2,1,0:T(8,128)} %bitcast.11, f32[3,128,128]{2,1,0:T(8,128)} %bitcast.13, f32[3,128,128]{2,1,0:T(8,128)} %bitcast.15, f32[128,128]{1,0:T(8,128)} %bitcast.17), custom_call_target="tpu_custom_call" | custom-call | tf_op jit(solution)/shard_map/edge_states/pallas_call | solution.py:316
  8.6 0.0 copy-start.1
  8.6 8.3 %collective-permute-start.1 = (f32[16,8,128]{2,1,0:T(8,128)}, f32[16,8,128]{2,1,0:T(8,128)S(1)}, u32[]{:S(2)}, u32[]{:S(2)}) collective-permute-start(f32[16,8,128]{2,1,0:T(8,128)} %get-tuple-element.23.first_ref), channel_id=1, source_target_pairs={{0,7},{1,0},{2,1},{3,2},{4,3},{5,4},{6,5},{7,6},{8,15},{9,8},{10,9... | collective-permute-start | bytes 196616 | tf_op jit(solution)/shard_map/ppermute | solution.py:847
  16.9 0.0 collective-permute-start
  17.5 0.0 copy-start.3
  17.6 3.8 %pair_sort.1 = (s32[2,128,128]{2,1,0:T(8,128)S(1)}, s32[8,128]{1,0:T(8,128)S(1)}) custom-call(s32[1,1]{1,0:T(1,128)} %bitcast.9.live_ref, s32[2,256,128]{2,1,0:T(8,128)S(1)} %bitcast.19), custom_call_target="tpu_custom_call" | custom-call | tf_op jit(solution)/shard_map/pair_sort/pallas_call | solution.py:419
  21.4 0.8 copy-done.7
  22.3 0.8 copy-done.8
  23.1 5.7 %inner_states.1.own_ref.table_ref = f32[128,8,128]{2,1,0:T(8,128)S(1)} custom-call(s32[24,128]{1,0:T(8,128)S(1)} %copy-done.6, s32[128,128]{1,0:T(8,128)S(1)} %copy-done.3, f32[3,128,256]{2,1,0:T(8,128)S(1)} %bitcast.12, f32[3,128,128]{2,1,0:T(8,128)S(1)} %bitcast.14, f32[3,128,128]{2,1,0:T(8,128)S(1)} %bitcast.16, f32[128,128]{1,0:T(8,128)S(1)} %bitcast.18, ...), custom_call_target="tpu_custom_call" | custom-call | tf_op jit(solution)/shard_map/inner_states/pallas_call | solution.py:361
  28.8 0.0 collective-permute-done.1.after_ref
  28.8 0.0 collective-permute-done.before_ref
  28.8 18.1 %pair_forces.1 = (f32[3,128,128]{2,1,0:T(8,128)S(1)}, f32[3,16,128]{2,1,0:T(8,128)S(1)}, f32[3,16,128]{2,1,0:T(8,128)S(1)}) custom-call(s32[1,1]{1,0:T(1,128)} %bitcast.10.live_ref, s32[8,128]{1,0:T(8,128)S(1)} %get-tuple-element.25.ends, s32[2,128,128]{2,1,0:T(8,128)S(1)} %get-tuple-element.26.keys_ref, f32[128,8,128]{2,1,0:T(8,128)S(1)} %inner_states.1.own_ref.table_ref, ...), custom_call_target="tpu_custom_call" | custom-call | tf_op jit(solution)/shard_map/pair_forces/pallas_call | solution.py:581
  46.9 4.6 %collective-permute-start.2 = (f32[3,16,128]{2,1,0:T(8,128)S(1)}, f32[3,16,128]{2,1,0:T(8,128)S(1)}, u32[]{:S(2)}, u32[]{:S(2)}) collective-permute-start(f32[3,16,128]{2,1,0:T(8,128)S(1)} %get-tuple-element.28), channel_id=1, source_target_pairs={{0,1},{1,2},{2,3},{3,4},{4,5},{5,6},{6,7},{7,0},{8,9},{9,10},{10,1... | collective-permute-start | bytes 73736 | tf_op jit(solution)/shard_map/ppermute | solution.py:847
  51.5 2.0 %collective-permute-start.3 = (f32[3,16,128]{2,1,0:T(8,128)S(1)}, f32[3,16,128]{2,1,0:T(8,128)S(1)}, u32[]{:S(2)}, u32[]{:S(2)}) collective-permute-start(f32[3,16,128]{2,1,0:T(8,128)S(1)} %get-tuple-element.29), channel_id=1, source_target_pairs={{0,7},{1,0},{2,1},{3,2},{4,3},{5,4},{6,5},{7,6},{8,15},{9,8},{10,9... | collective-permute-start | bytes 73736 | tf_op jit(solution)/shard_map/ppermute | solution.py:847
  53.5 4.1 %inner_deposit.1.inner_ref = f32[6,144,128]{2,1,0:T(8,128)S(1)} custom-call(s32[24,128]{1,0:T(8,128)S(1)} %copy-done.6, s32[128,128]{1,0:T(8,128)S(1)} %copy-done.3, f32[128,8,128]{2,1,0:T(8,128)S(1)} %inner_states.1.own_ref.table_ref, f32[3,128,128]{2,1,0:T(8,128)S(1)} %get-tuple-element.27.corr_ref), custom_call_target="tpu_custom_call" | custom-call | tf_op jit(solution)/shard_map/inner_deposit/pallas_call | solution.py:704
  57.6 1.4 %collective-permute-done.3.upper_ref = f32[3,16,128]{2,1,0:T(8,128)S(1)} collective-permute-done((f32[3,16,128]{2,1,0:T(8,128)S(1)}, f32[3,16,128]{2,1,0:T(8,128)S(1)}, u32[]{:S(2)}, u32[]{:S(2)}) %collective-permute-start.3) | collective-permute-done | bytes 24608 | tf_op jit(solution)/shard_map/ppermute | solution.py:847
  59.0 2.8 %edge_deposit.1 = (f32[3,128,256]{2,1,0:T(8,128)S(1)}, f32[3,128,128]{2,1,0:T(8,128)}, f32[3,32,256]{2,1,0:T(8,128)S(1)}, f32[3,32,256]{2,1,0:T(8,128)S(1)}) custom-call(s32[24,128]{1,0:T(8,128)S(1)} %copy-done.6, s32[128,128]{1,0:T(8,128)S(1)} %copy-done.3, f32[128,8,128]{2,1,0:T(8,128)S(1)} %inner_states.1.own_ref.table_ref, ...), custom_call_target="tpu_custom_call" | custom-call | tf_op jit(solution)/shard_map/edge_deposit/pallas_call | solution.py:743
  61.8 1.6 %collective-permute-start.4 = (f32[3,32,256]{2,1,0:T(8,128)S(1)}, f32[3,32,256]{2,1,0:T(8,128)S(1)}, u32[]{:S(2)}, u32[]{:S(2)}) collective-permute-start(f32[3,32,256]{2,1,0:T(8,128)S(1)} %get-tuple-element.32), channel_id=1, source_target_pairs={{0,64},{64,128},{128,192},{1,65},{65,129},{129,193},{2,66},{66,130... | collective-permute-start | bytes 294920 | tf_op jit(solution)/shard_map/ppermute | solution.py:847
  63.5 1.3 %collective-permute-start.5 = (f32[3,32,256]{2,1,0:T(8,128)S(1)}, f32[3,32,256]{2,1,0:T(8,128)S(1)}, u32[]{:S(2)}, u32[]{:S(2)}) collective-permute-start(f32[3,32,256]{2,1,0:T(8,128)S(1)} %get-tuple-element.33), channel_id=1, source_target_pairs={{64,0},{128,64},{192,128},{65,1},{129,65},{193,129},{66,2},{130,66... | collective-permute-start | bytes 294920 | tf_op jit(solution)/shard_map/ppermute | solution.py:847
  64.8 0.3 collective-permute-done.4.before_ref
  65.1 3.7 %collective-permute-done.5.after_ref = f32[3,32,256]{2,1,0:T(8,128)S(1)} collective-permute-done((f32[3,32,256]{2,1,0:T(8,128)S(1)}, f32[3,32,256]{2,1,0:T(8,128)S(1)}, u32[]{:S(2)}, u32[]{:S(2)}) %collective-permute-start.5) | collective-permute-done | bytes 98336 | tf_op jit(solution)/shard_map/ppermute | solution.py:847
  68.8 0.1 axial_filter.1
  69.0 7.1 %collective-permute-start.6 = (f32[3,16,256]{2,1,0:T(8,128)S(1)}, f32[3,16,256]{2,1,0:T(8,128)S(1)}, u32[]{:S(2)}, u32[]{:S(2)}) collective-permute-start(f32[3,16,256]{2,1,0:T(8,128)S(1)} %get-tuple-element.35), channel_id=1, source_target_pairs={{0,8},{8,16},{16,24},{24,32},{32,40},{40,48},{48,56},{1,9},{9,17},... | collective-permute-start | bytes 147464 | tf_op jit(solution)/shard_map/ppermute | solution.py:847
  76.0 1.9 %collective-permute-start.7 = (f32[3,16,256]{2,1,0:T(8,128)S(1)}, f32[3,16,256]{2,1,0:T(8,128)S(1)}, u32[]{:S(2)}, u32[]{:S(2)}) collective-permute-start(f32[3,16,256]{2,1,0:T(8,128)S(1)} %get-tuple-element.36), channel_id=1, source_target_pairs={{8,0},{16,8},{24,16},{32,24},{40,32},{48,40},{56,48},{9,1},{17,9},... | collective-permute-start | bytes 147464 | tf_op jit(solution)/shard_map/ppermute | solution.py:847
  78.0 0.0 collective-permute-done.6.before_ref
  78.0 3.5 %collective-permute-done.7.after_ref = f32[3,16,256]{2,1,0:T(8,128)S(1)} collective-permute-done((f32[3,16,256]{2,1,0:T(8,128)S(1)}, f32[3,16,256]{2,1,0:T(8,128)S(1)}, u32[]{:S(2)}, u32[]{:S(2)}) %collective-permute-start.7) | collective-permute-done | bytes 49184 | tf_op jit(solution)/shard_map/ppermute | solution.py:847
  81.4 0.5 radial_filter.1
  82.0 3.0 %collective-permute-start.8 = (f32[8,128]{1,0:T(8,128)S(1)}, f32[8,128]{1,0:T(8,128)S(1)}, u32[]{:S(2)}, u32[]{:S(2)}) collective-permute-start(f32[8,128]{1,0:T(8,128)S(1)} %get-tuple-element.38), channel_id=1, source_target_pairs={{0,1},{1,2},{2,3},{3,4},{4,5},{5,6},{6,7},{7,0},{8,9},{9,10},{10,1... | collective-permute-start | bytes 12296 | tf_op jit(solution)/shard_map/ppermute | solution.py:847
  85.0 3.3 %collective-permute-start.9 = (f32[8,128]{1,0:T(8,128)S(1)}, f32[8,128]{1,0:T(8,128)S(1)}, u32[]{:S(2)}, u32[]{:S(2)}) collective-permute-start(f32[8,128]{1,0:T(8,128)S(1)} %get-tuple-element.39), channel_id=1, source_target_pairs={{0,7},{1,0},{2,1},{3,2},{4,3},{5,4},{6,5},{7,6},{8,15},{9,8},{10,9... | collective-permute-start | bytes 12296 | tf_op jit(solution)/shard_map/ppermute | solution.py:847
  88.3 1.0 %collective-permute-done.8.before_ref = f32[8,128]{1,0:T(8,128)S(1)} collective-permute-done((f32[8,128]{1,0:T(8,128)S(1)}, f32[8,128]{1,0:T(8,128)S(1)}, u32[]{:S(2)}, u32[]{:S(2)}) %collective-permute-start.8) | collective-permute-done | bytes 4128 | tf_op jit(solution)/shard_map/ppermute | solution.py:847
  89.3 2.0 %collective-permute-done.9.after_ref = f32[8,128]{1,0:T(8,128)S(1)} collective-permute-done((f32[8,128]{1,0:T(8,128)S(1)}, f32[8,128]{1,0:T(8,128)S(1)}, u32[]{:S(2)}, u32[]{:S(2)}) %collective-permute-start.9) | collective-permute-done | bytes 4128 | tf_op jit(solution)/shard_map/ppermute | solution.py:847
  91.3 1.6 %azimuthal_filter.1 = f32[3,128,256]{2,1,0:T(8,128)} custom-call(f32[3,128,256]{2,1,0:T(8,128)S(1)} %get-tuple-element.37.cells_ref, f32[8,128]{1,0:T(8,128)S(1)} %collective-permute-done.8.before_ref, f32[8,128]{1,0:T(8,128)S(1)} %collective-permute-done.9.after_ref), custom_call_target="tpu_custom_call" | custom-call | tf_op jit(solution)/shard_map/azimuthal_filter/pallas_call | solution.py:836
  (15 shorter events, 0.0 us)
Async XLA Ops:
  0.6 16.9 %copy-start.5 = (s32[2,1,1,32768]{3,2,1,0:T(1,128)S(1)}, s32[2,1,1,32768]{3,2,1,0:T(1,128)}, u32[]{:S(2)}) copy-start(s32[2,1,1,32768]{3,2,1,0:T(1,128)} %param.11) | copy-start | bytes 786436
  0.6 20.7 %copy-start = (f32[3,8,16,256]{3,2,1,0:T(8,128)S(1)}, f32[3,8,16,256]{3,2,1,0:T(8,128)}, u32[]{:S(2)}) copy-start(f32[3,8,16,256]{3,2,1,0:T(8,128)} %param.13) | copy-start | bytes 1179652
  0.7 20.7 %copy-start.2 = (f32[3,1,1,16384]{3,2,1,0:T(1,128)S(1)}, f32[3,1,1,16384]{3,2,1,0:T(1,128)}, u32[]{:S(2)}) copy-start(f32[3,1,1,16384]{3,2,1,0:T(1,128)} %param.8) | copy-start | bytes 589828
  0.7 20.7 %copy-start.4 = (f32[1,1,16384]{2,1,0:T(1,128)S(1)}, f32[1,1,16384]{2,1,0:T(1,128)}, u32[]{:S(2)}) copy-start(f32[1,1,16384]{2,1,0:T(1,128)} %param.9) | copy-start | bytes 196612
  8.6 12.8 %copy-start.1 = (f32[3,1,1,16384]{3,2,1,0:T(1,128)S(1)}, f32[3,1,1,16384]{3,2,1,0:T(1,128)}, u32[]{:S(2)}) copy-start(f32[3,1,1,16384]{3,2,1,0:T(1,128)} %param.7) | copy-start | bytes 589828
  8.6 20.2 %collective-permute-start.1 = (f32[16,8,128]{2,1,0:T(8,128)}, f32[16,8,128]{2,1,0:T(8,128)S(1)}, u32[]{:S(2)}, u32[]{:S(2)}) collective-permute-start(f32[16,8,128]{2,1,0:T(8,128)} %get-tuple-element.23.first_ref), channel_id=1, source_target_pairs={{0,7},{1,0},{2,1},{3,2},{4,3},{5,4},{6,5},{7,6},{8,15},{9,8},{10,9... | collective-permute-start | bytes 196616 | tf_op jit(solution)/shard_map/ppermute | solution.py:847
  16.9 11.9 %collective-permute-start = (f32[16,8,128]{2,1,0:T(8,128)}, f32[16,8,128]{2,1,0:T(8,128)S(1)}, u32[]{:S(2)}, u32[]{:S(2)}) collective-permute-start(f32[16,8,128]{2,1,0:T(8,128)} %get-tuple-element.24.last_ref), channel_id=1, source_target_pairs={{0,1},{1,2},{2,3},{3,4},{4,5},{5,6},{6,7},{7,0},{8,9},{9,10},{10,1... | collective-permute-start | bytes 196616 | tf_op jit(solution)/shard_map/ppermute | solution.py:847
  17.5 3.8 %copy-start.3 = (s32[128,128]{1,0:T(8,128)S(1)}, s32[128,128]{1,0:T(8,128)}, u32[]{:S(2)}) copy-start(s32[128,128]{1,0:T(8,128)} %get-tuple-element.22.keys_ref) | copy-start | bytes 196612
  17.6 3.8 %copy-start.6 = (s32[24,128]{1,0:T(8,128)S(1)}, s32[24,128]{1,0:T(8,128)}, u32[]{:S(2)}) copy-start(s32[24,128]{1,0:T(8,128)} %get-tuple-element.21.ends) | copy-start | bytes 36868
  21.4 0.8 copy-start.7
  22.2 0.8 copy-start.8
  46.9 10.7 %collective-permute-start.2 = (f32[3,16,128]{2,1,0:T(8,128)S(1)}, f32[3,16,128]{2,1,0:T(8,128)S(1)}, u32[]{:S(2)}, u32[]{:S(2)}) collective-permute-start(f32[3,16,128]{2,1,0:T(8,128)S(1)} %get-tuple-element.28), channel_id=1, source_target_pairs={{0,1},{1,2},{2,3},{3,4},{4,5},{5,6},{6,7},{7,0},{8,9},{9,10},{10,1... | collective-permute-start | bytes 73736 | tf_op jit(solution)/shard_map/ppermute | solution.py:847
  51.5 7.5 %collective-permute-start.3 = (f32[3,16,128]{2,1,0:T(8,128)S(1)}, f32[3,16,128]{2,1,0:T(8,128)S(1)}, u32[]{:S(2)}, u32[]{:S(2)}) collective-permute-start(f32[3,16,128]{2,1,0:T(8,128)S(1)} %get-tuple-element.29), channel_id=1, source_target_pairs={{0,7},{1,0},{2,1},{3,2},{4,3},{5,4},{6,5},{7,6},{8,15},{9,8},{10,9... | collective-permute-start | bytes 73736 | tf_op jit(solution)/shard_map/ppermute | solution.py:847
  61.8 3.3 %collective-permute-start.4 = (f32[3,32,256]{2,1,0:T(8,128)S(1)}, f32[3,32,256]{2,1,0:T(8,128)S(1)}, u32[]{:S(2)}, u32[]{:S(2)}) collective-permute-start(f32[3,32,256]{2,1,0:T(8,128)S(1)} %get-tuple-element.32), channel_id=1, source_target_pairs={{0,64},{64,128},{128,192},{1,65},{65,129},{129,193},{2,66},{66,130... | collective-permute-start | bytes 294920 | tf_op jit(solution)/shard_map/ppermute | solution.py:847
  63.5 5.4 %collective-permute-start.5 = (f32[3,32,256]{2,1,0:T(8,128)S(1)}, f32[3,32,256]{2,1,0:T(8,128)S(1)}, u32[]{:S(2)}, u32[]{:S(2)}) collective-permute-start(f32[3,32,256]{2,1,0:T(8,128)S(1)} %get-tuple-element.33), channel_id=1, source_target_pairs={{64,0},{128,64},{192,128},{65,1},{129,65},{193,129},{66,2},{130,66... | collective-permute-start | bytes 294920 | tf_op jit(solution)/shard_map/ppermute | solution.py:847
  69.0 9.0 %collective-permute-start.6 = (f32[3,16,256]{2,1,0:T(8,128)S(1)}, f32[3,16,256]{2,1,0:T(8,128)S(1)}, u32[]{:S(2)}, u32[]{:S(2)}) collective-permute-start(f32[3,16,256]{2,1,0:T(8,128)S(1)} %get-tuple-element.35), channel_id=1, source_target_pairs={{0,8},{8,16},{16,24},{24,32},{32,40},{40,48},{48,56},{1,9},{9,17},... | collective-permute-start | bytes 147464 | tf_op jit(solution)/shard_map/ppermute | solution.py:847
  76.0 5.4 %collective-permute-start.7 = (f32[3,16,256]{2,1,0:T(8,128)S(1)}, f32[3,16,256]{2,1,0:T(8,128)S(1)}, u32[]{:S(2)}, u32[]{:S(2)}) collective-permute-start(f32[3,16,256]{2,1,0:T(8,128)S(1)} %get-tuple-element.36), channel_id=1, source_target_pairs={{8,0},{16,8},{24,16},{32,24},{40,32},{48,40},{56,48},{9,1},{17,9},... | collective-permute-start | bytes 147464 | tf_op jit(solution)/shard_map/ppermute | solution.py:847
  82.0 7.3 %collective-permute-start.8 = (f32[8,128]{1,0:T(8,128)S(1)}, f32[8,128]{1,0:T(8,128)S(1)}, u32[]{:S(2)}, u32[]{:S(2)}) collective-permute-start(f32[8,128]{1,0:T(8,128)S(1)} %get-tuple-element.38), channel_id=1, source_target_pairs={{0,1},{1,2},{2,3},{3,4},{4,5},{5,6},{6,7},{7,0},{8,9},{9,10},{10,1... | collective-permute-start | bytes 12296 | tf_op jit(solution)/shard_map/ppermute | solution.py:847
  85.0 6.4 %collective-permute-start.9 = (f32[8,128]{1,0:T(8,128)S(1)}, f32[8,128]{1,0:T(8,128)S(1)}, u32[]{:S(2)}, u32[]{:S(2)}) collective-permute-start(f32[8,128]{1,0:T(8,128)S(1)} %get-tuple-element.39), channel_id=1, source_target_pairs={{0,7},{1,0},{2,1},{3,2},{4,3},{5,4},{6,5},{7,6},{8,15},{9,8},{10,9... | collective-permute-start | bytes 12296 | tf_op jit(solution)/shard_map/ppermute | solution.py:847
